TPU v7x, 128 devices: a whole 4x4x4 slice. The times are simulated.
128 devices in a mesh: tm: 4 (over y_hi, core), height: 4 (over z), head: 8 (over x, y_lo).
Axes of the slice: x: 4, y: 4 (y_hi: 2, y_lo: 2; y = y_hi * 2 + y_lo), z: 4, core: 2. Of those that a mesh axis runs over, the one named last changes fastest.
Arguments:
- queries: bfloat16 [8, 4, 4, 4, 256, 128], P('head', 'tm', 'height'), may hold values from -8 to 8
- key_tiles: bfloat16 [8, 4, 4, 4, 256, 128], P('head', 'tm', 'height'), may hold values from -8 to 8
- values: bfloat16 [8, 4, 4, 4, 256, 128], P('head', 'tm', 'height'), may hold values from -6 to 6
- token_valid: int32 [4, 4, 4, 256], replicated, may hold values from 0 to 1, as said below
- out_weight: bfloat16 [1536, 1024], P(None, 'head'), may hold values from -2.5 to 2.5
- out_grad: bfloat16 [1536, 4, 4, 4, 256], P(None, 'tm', 'height'), may hold values from -2 to 2
Outputs:
- mixed: bfloat16 [1536, 4, 4, 4, 256], P('head', 'tm', 'height')
- query_grad: bfloat16 [8, 4, 4, 4, 256, 128], P('head', 'tm', 'height')
- key_grad: bfloat16 [8, 4, 4, 4, 256, 128], P('head', 'tm', 'height')
- value_grad: bfloat16 [8, 4, 4, 4, 256, 128], P('head', 'tm', 'height')
- weight_grad: float32 [1536, 1024], P(('tm', 'height'), 'head')
Inputs may be any that keep to these rules, and one draw needn't show every extreme that they name: `token_valid`: A token is valid when its frame lies below the clip's frame extent, at least 13; its row below its frame's own row extent, from 25 to 31; and its column below its frame's and row's own column extent, from 25 to 31.
All inputs are finite; a program needn't handle non-finite values.
Results may differ from a plain program's by a relative error of at most 0.025.
Values may be sent and summed in bfloat16 or wider, within the bound.
A program may use at most 192 MiB of HBM per device.

v0:
```python
import math

import jax
import jax.numpy as jnp
from jax import lax
from jax.sharding import PartitionSpec as P

masked_score = -1e30


def padded(block, sides, width):
    for axis, dim in sides:
        count = lax.axis_size(axis)
        forward = [(i, i + 1) for i in range(count - 1)]
        backward = [(target, source) for source, target in forward]
        low = lax.ppermute(
            lax.slice_in_dim(block, block.shape[dim] - width, None, axis=dim), axis, forward
        )
        high = lax.ppermute(lax.slice_in_dim(block, 0, width, axis=dim), axis, backward)
        block = jnp.concatenate([low, block, high], axis=dim)
    return block


def passed_along(value, axis, by):
    size = lax.axis_size(axis)
    pairs = [(i, i + by) for i in range(size) if 0 <= i + by < size]
    return lax.ppermute(value, axis, pairs)


def for_sending(value):
    return jax.tree.map(lambda a: a.astype(jnp.bfloat16) if a.dtype == jnp.float32 else a, value)


def per_device(queries, key_tiles, values, token_valid, out_weight, out_grad):
    heads_here = queries.shape[0]
    span_cols = queries.shape[3]
    tile_tokens = queries.shape[4]
    head_size = queries.shape[5]
    model_width = out_weight.shape[0]
    factor = 1.0 / math.sqrt(head_size)
    stacked = jnp.stack([key_tiles, values])
    beside_all = padded(stacked, (("tm", 2), ("height", 3)), 1)
    beside_all = jnp.pad(beside_all, ((0, 0), (0, 0), (0, 0), (0, 0), (1, 1), (0, 0), (0, 0)))
    near_cols = jnp.transpose(beside_all, (0, 1, 4, 2, 3, 5, 6)).reshape(
        2, heads_here, span_cols + 2, 9 * tile_tokens, head_size
    )
    frame_index = lax.axis_index("tm")
    row_index = lax.axis_index("height")
    anchor = jnp.zeros((), jnp.int32)
    valid_pad = jnp.pad(token_valid, ((1, 1), (1, 1), (1, 1), (0, 0)))
    near_valid = lax.dynamic_slice(
        valid_pad, (frame_index, row_index, anchor, anchor), (3, 3, span_cols + 2, tile_tokens)
    )
    near_ok = jnp.transpose(near_valid, (2, 0, 1, 3)).reshape(span_cols + 2, 9 * tile_tokens) > 0
    query_here = queries.reshape(heads_here, span_cols, tile_tokens, head_size)

    def block_scores(query_head, key_cols, offset):
        key_part = key_cols[offset : offset + span_cols]
        scores = (
            jnp.einsum("cne,cme->cnm", query_head, key_part, preferred_element_type=jnp.float32)
            * factor
        )
        part_ok = near_ok[offset : offset + span_cols][:, None, :]
        return (jnp.where(part_ok, scores, masked_score), part_ok)

    def forward_head(operands):
        query_head, key_cols, value_cols = operands
        block_tops = []
        block_totals = []
        for offset in range(3):
            scores, part_ok = block_scores(query_head, key_cols, offset)
            highest = jnp.max(scores, axis=-1, keepdims=True)
            block_tops.append(highest)
            block_totals.append(
                jnp.sum(jnp.where(part_ok, jnp.exp(scores - highest), 0.0), axis=-1, keepdims=True)
            )
        overall = jnp.maximum(jnp.maximum(block_tops[0], block_tops[1]), block_tops[2])
        grand_total = block_totals[0] * jnp.exp(block_tops[0] - overall)
        grand_total = grand_total + block_totals[1] * jnp.exp(block_tops[1] - overall)
        grand_total = grand_total + block_totals[2] * jnp.exp(block_tops[2] - overall)
        log_total = overall + jnp.log(grand_total)
        attended = jnp.zeros((span_cols, tile_tokens, head_size), jnp.float32)
        for offset in range(3):
            scores, part_ok = block_scores(query_head, key_cols, offset)
            weights = jnp.where(part_ok, jnp.exp(scores - log_total), 0.0).astype(jnp.bfloat16)
            attended = attended + jnp.einsum(
                "cnm,cme->cne",
                weights,
                value_cols[offset : offset + span_cols],
                preferred_element_type=jnp.float32,
            )
        return (attended.astype(jnp.bfloat16), log_total)

    attended, log_sum = lax.map(forward_head, (query_here, near_cols[0], near_cols[1]))
    weight_heads = out_weight.reshape(model_width, heads_here, head_size)
    mixed = lax.psum_scatter(
        jnp.einsum(
            "dhe,hcne->dcn", weight_heads, attended, preferred_element_type=jnp.float32
        ).astype(jnp.bfloat16),
        "head",
        scatter_dimension=0,
        tiled=True,
    ).astype(jnp.float32)
    mixed = mixed.astype(jnp.bfloat16).reshape(mixed.shape[0], 1, 1, span_cols, tile_tokens)
    grad_rows = out_grad.reshape(model_width, span_cols, tile_tokens)
    grad_attended = jnp.einsum(
        "dcn,dhe->hcne", grad_rows, weight_heads, preferred_element_type=jnp.float32
    ).astype(jnp.bfloat16)
    row_delta = jnp.sum(
        grad_attended.astype(jnp.float32) * attended.astype(jnp.float32), axis=-1, keepdims=True
    )
    product = jnp.einsum("dcn,hcne->dhe", grad_rows, attended, preferred_element_type=jnp.float32)
    weight_grad = lax.psum_scatter(
        product.reshape(
            lax.axis_size(("tm", "height")) * (model_width // lax.axis_size(("tm", "height"))),
            heads_here * head_size,
        ).astype(jnp.bfloat16),
        ("tm", "height"),
        scatter_dimension=0,
        tiled=True,
    ).astype(jnp.float32)
    tile_shape = (heads_here, 1, 1, span_cols, tile_tokens, head_size)

    def backward_head(operands):
        query_head, key_cols, value_cols, grad_head, total_head, delta_head = operands
        query_sum = jnp.zeros((span_cols, tile_tokens, head_size), jnp.float32)
        key_back = jnp.zeros((span_cols + 2, 9 * tile_tokens, head_size), jnp.float32)
        value_back = jnp.zeros((span_cols + 2, 9 * tile_tokens, head_size), jnp.float32)
        for offset in range(3):
            scores, part_ok = block_scores(query_head, key_cols, offset)
            probs = jnp.where(part_ok, jnp.exp(scores - total_head), 0.0)
            grad_probs = jnp.einsum(
                "cne,cme->cnm",
                grad_head,
                value_cols[offset : offset + span_cols],
                preferred_element_type=jnp.float32,
            )
            grad_scores = (probs * (grad_probs - delta_head)).astype(jnp.bfloat16)
            query_sum = query_sum + jnp.einsum(
                "cnm,cme->cne",
                grad_scores,
                key_cols[offset : offset + span_cols],
                preferred_element_type=jnp.float32,
            )
            key_part = (
                jnp.einsum(
                    "cnm,cne->cme", grad_scores, query_head, preferred_element_type=jnp.float32
                )
                * factor
            )
            value_part = jnp.einsum(
                "cnm,cne->cme",
                probs.astype(jnp.bfloat16),
                grad_head,
                preferred_element_type=jnp.float32,
            )
            key_back = key_back.at[offset : offset + span_cols].add(key_part)
            value_back = value_back.at[offset : offset + span_cols].add(value_part)
        return ((query_sum * factor).astype(jnp.bfloat16), key_back, value_back)

    query_grad, key_back, value_back = lax.map(
        backward_head, (query_here, near_cols[0], near_cols[1], grad_attended, log_sum, row_delta)
    )
    returned = jnp.stack([key_back, value_back])
    returned = returned.reshape(2, heads_here, span_cols + 2, 3, 3, tile_tokens, head_size)[
        :, :, 1:-1
    ]
    returned = jnp.transpose(returned, (0, 1, 3, 4, 2, 5, 6))
    lead_up = passed_along(returned[:, :, 2].astype(jnp.bfloat16), "tm", 1).astype(jnp.float32)
    lead_down = passed_along(returned[:, :, 0].astype(jnp.bfloat16), "tm", -1).astype(jnp.float32)
    merged = returned[:, :, 1] + lead_up + lead_down
    trail_up = passed_along(for_sending(merged[:, :, 2]), "height", 1)
    trail_down = passed_along(for_sending(merged[:, :, 0]), "height", -1)
    combined = merged[:, :, 1] + trail_up + trail_down
    key_grad = combined[0].astype(jnp.bfloat16).reshape(tile_shape)
    value_grad = combined[1].astype(jnp.bfloat16).reshape(tile_shape)
    return (mixed, query_grad.reshape(tile_shape), key_grad, value_grad, weight_grad)


def solution(mesh):
    placed = (
        P("head", "tm", "height", None, None, None),
        P("head", "tm", "height", None, None, None),
        P("head", "tm", "height", None, None, None),
        P(),
        P(None, "head"),
        P(None, "tm", "height", None, None),
    )
    return jax.shard_map(
        per_device,
        mesh=mesh,
        in_specs=placed,
        out_specs=(
            P("head", "tm", "height", None, None),
            P("head", "tm", "height", None, None, None),
            P("head", "tm", "height", None, None, None),
            P("head", "tm", "height", None, None, None),
            P(("tm", "height"), "head"),
        ),
        check_vma=False,
    )
```

profile of v0, /device:TPU:1, one launch (start us, length us, event | category | flops | bytes accessed | tf_op | source)
XLA Modules:
  0.0 349.3 jit_solution(1735895394015377330)
XLA Ops:
  9.3 3.3 collective-permute-start.1
  12.6 4.8 %collective-permute-start = (bf16[2,1,1,1,4,256,128]{6,5,3,2,4,1,0:T(8,128)(2,1)S(1)}, bf16[2,1,1,1,4,256,128]{6,5,3,2,4,1,0:T(8,128)(2,1)S(1)}, u32[]{:S(2)}, u32[]{:S(2)}) collective-permute-start(bf16[2,1,1,1,4,256,128]{6,5,3,2,4,1,0:T(8,128)(2,1)S(1)} %pad_maximum_fusion.2), channel_id=1, source_target_pairs={{0,32},{32,64},{64,96},{1,33},{33,65},{65,97},{2,34},{34,66},{66,9... | collective-permute-start | bytes 1572872 | tf_op jit(solution)/shard_map/ppermute | solution.py:16
  17.5 4.9 %collective-permute-done.1 = bf16[2,1,1,1,4,256,128]{6,5,3,2,4,1,0:T(8,128)(2,1)S(1)} collective-permute-done((bf16[2,1,1,1,4,256,128]{6,5,3,2,4,1,0:T(8,128)(2,1)S(1)}, bf16[2,1,1,1,4,256,128]{6,5,3,2,4,1,0:T(8,128)(2,1)S(1)}, u32[]{:S(2)}, u32[]{:S(2)}) %collective-permute-start.1) | collective-permute-done | bytes 524320 | tf_op jit(solution)/shard_map/ppermute | solution.py:19
  27.4 5.3 %collective-permute-start.2 = (bf16[2,1,3,1,4,256,128]{6,5,3,2,4,1,0:T(8,128)(2,1)}, bf16[2,1,3,1,4,256,128]{6,5,3,2,4,1,0:T(8,128)(2,1)}, u32[]{:S(2)}, u32[]{:S(2)}) collective-permute-start(bf16[2,1,3,1,4,256,128]{6,5,3,2,4,1,0:T(8,128)(2,1)} %pad_maximum_fusion.1), channel_id=1, source_target_pairs={{0,8},{8,16},{16,24},{1,9},{9,17},{17,25},{2,10},{10,18},{18,26},{... | collective-permute-start | bytes 4718600 | tf_op jit(solution)/shard_map/ppermute | solution.py:16
  35.2 22.8 %collective-permute-done.3 = bf16[2,1,3,1,4,256,128]{6,5,3,2,4,1,0:T(8,128)(2,1)} collective-permute-done((bf16[2,1,3,1,4,256,128]{6,5,3,2,4,1,0:T(8,128)(2,1)}, bf16[2,1,3,1,4,256,128]{6,5,3,2,4,1,0:T(8,128)(2,1)}, u32[]{:S(2)}, u32[]{:S(2)}) %collective-permute-start.3) | collective-permute-done | bytes 1572896 | tf_op jit(solution)/shard_map/ppermute | solution.py:19
  59.7 4.9 %fusion.19 = bf16[2,1,6,3,3,256,128]{6,5,4,3,2,1,0:T(8,128)(2,1)S(1)} fusion(bf16[2,1,3,1,4,256,128]{6,5,3,2,4,1,0:T(8,128)(2,1)} %collective-permute-done.3, bf16[2,1,3,1,4,256,128]{6,5,3,2,4,1,0:T(8,128)(2,1)} %collective-permute-done.2, bf16[2,1,1,1,4,256,128]{6,5,3,2,4,1,0:T(8,128)(2,1)} %copy-done.13, ...), kind=kLoop, calls=%fused_computation.39 | loop fusion | flops 74317824 | bytes 11796480 | tf_op jit(solution)/shard_map/transpose | solution.py:44
  64.6 3.2 fusion.99
  67.9 4.9 %bitcast_reduce_fusion = (f32[4,256]{1,0:T(4,128)S(1)}, f32[4,2304,256]{2,1,0:T(8,128)S(1)}) fusion(bf16[4,2304,128]{2,1,0:T(8,128)(2,1)S(1)} %bitcast.228, bf16[1,1,1,4,256,128]{5,4,3,2,1,0:T(8,128)(2,1)S(1)} %copy-done.8, pred[4,2304]{1,0:T(4,128)(4,1)S(1)} %bitcast.247), kind=kOutput, calls=%fused_computation.7 | convolution fusion | flops 611056640 | bytes 12071936 | tf_op jit(solution)/shard_map/while/body/eval_jaxpr/cne,cme->cnm/dot_general | solution.py:60
  72.8 4.9 %bitcast_reduce_fusion.1 = (f32[4,256]{1,0:T(4,128)S(1)}, f32[4,2304,256]{2,1,0:T(8,128)S(1)}) fusion(bf16[4,2304,128]{2,1,0:T(8,128)(2,1)S(1)} %bitcast.226, bf16[1,1,1,4,256,128]{5,4,3,2,1,0:T(8,128)(2,1)S(1)} %copy-done.8, pred[4,2304]{1,0:T(4,128)(4,1)S(1)} %bitcast.252), kind=kOutput, calls=%fused_computation.15 | convolution fusion | flops 611056640 | bytes 12071936 | tf_op jit(solution)/shard_map/while/body/eval_jaxpr/cne,cme->cnm/dot_general | solution.py:60
  77.7 4.9 %bitcast_reduce_fusion.2 = (f32[4,256]{1,0:T(4,128)S(1)}, f32[4,2304,256]{2,1,0:T(8,128)S(1)}) fusion(bf16[4,2304,128]{2,1,0:T(8,128)(2,1)S(1)} %bitcast.224, bf16[1,1,1,4,256,128]{5,4,3,2,1,0:T(8,128)(2,1)S(1)} %copy-done.8, pred[4,2304]{1,0:T(4,128)(4,1)S(1)} %bitcast.242), kind=kOutput, calls=%fused_computation.23 | convolution fusion | flops 611056640 | bytes 12071936 | tf_op jit(solution)/shard_map/while/body/eval_jaxpr/cne,cme->cnm/dot_general | solution.py:60
  84.7 6.2 %fusion.3 = (f32[4,256]{1,0:T(4,128)S(1)}, f32[4,256]{1,0:T(4,128)S(1)}) fusion(f32[4,2304,256]{2,1,0:T(8,128)S(1)} %get-tuple-element.194, f32[4,256]{1,0:T(4,128)S(1)} %get-tuple-element.193, pred[4,2304]{1,0:T(4,128)(4,1)S(1)} %bitcast.248, f32[4,256]{1,0:T(4,128)S(1)} %get-tuple-element.195, f32[4,2304,256]{2,1,0:T(8,128)S(1)} %get-tuple-element.196, ...), kind=kLoop, calls=%fused_computation.10 | loop fusion | flops 14153728 | bytes 18909184 | tf_op jit(solution)/shard_map/while/body/eval_jaxpr/reduce_sum | solution.py:75
  91.0 3.1 fusion.65
  94.1 5.9 %fusion.68 = f32[4,256,128]{1,2,0:T(8,128)S(1)} fusion(bf16[4,2304,128]{2,1,0:T(8,128)(2,1)S(1)} %bitcast.232, f32[4,2304,256]{2,1,0:T(8,128)} %copy-done.1, f32[4,256]{1,0:T(4,128)S(1)} %log_add_fusion, pred[4,2304]{1,0:T(4,128)(4,1)S(1)} %bitcast.254), kind=kOutput, calls=%fused_computation.91 | convolution fusion | flops 611057664 | bytes 12334080 | tf_op jit(solution)/shard_map/while/body/eval_jaxpr/cnm,cme->cne/dot_general | solution.py:86
  100.1 3.8 %fusion.73 = (f32[4,256]{1,0:T(4,128)S(1)}, bf16[4,256,128]{1,2,0:T(8,128)(2,1)}) fusion(bf16[128,4,256]{2,0,1:T(8,128)(2,1)S(1)} %fusion.56, f32[4,256,128]{1,2,0:T(8,128)S(1)} %fusion.65, f32[4,256,128]{1,2,0:T(8,128)S(1)} %fusion.68, bf16[4,2304,128]{2,1,0:T(8,128)(2,1)S(1)} %bitcast.230, f32[4,2304,256]{2,1,0:T(8,128)S(1)} %get-tuple-element.198, ...), kind=kOutput, calls=%fused_computation.97 | convolution fusion | flops 611974144 | bytes 13386752 | tf_op jit(solution)/shard_map/while/body/eval_jaxpr/cnm,cme->cne/dot_general | solution.py:86
  103.9 4.6 %multiply_convert_fusion = bf16[4,256,2304]{1,2,0:T(8,128)(2,1)} fusion(f32[4,2304,256]{2,1,0:T(8,128)S(1)} %get-tuple-element.194, bf16[4,2304,128]{2,1,0:T(8,128)(2,1)S(1)} %bitcast.235, f32[4,256]{1,0:T(4,128)S(1)} %get-tuple-element.199, f32[4,256]{1,0:T(4,128)S(1)} %log_add_fusion, pred[4,2304]{1,0:T(4,128)(4,1)S(1)} %bitcast.250, ...), kind=kOutput, calls=%fused_computation.29 | convolution fusion | flops 615776256 | bytes 16794624 | tf_op jit(solution)/shard_map/while/body/eval_jaxpr/cne,cme->cnm/dot_general | solution.py:132
  108.6 9.0 %multiply_convert_fusion.1 = bf16[4,256,2304]{1,2,0:T(8,128)(2,1)} fusion(f32[4,2304,256]{2,1,0:T(8,128)} %copy-done.1, bf16[4,2304,128]{2,1,0:T(8,128)(2,1)S(1)} %bitcast.233, f32[4,256]{1,0:T(4,128)S(1)} %get-tuple-element.199, f32[4,256]{1,0:T(4,128)S(1)} %log_add_fusion, pred[4,2304]{1,0:T(4,128)(4,1)S(1)} %bitcast.255, bf16[128,4,256]{2,0,1:T(8,128)(2,1)S(1)} %fusion.56), kind=kOutput, calls=%fused_computation.30 | convolution fusion | flops 615776256 | bytes 16794624 | tf_op jit(solution)/shard_map/while/body/eval_jaxpr/cne,cme->cnm/dot_general | solution.py:132
  123.5 7.5 %fusion.27 = f32[6,2304,128]{2,1,0:T(8,128)S(1)} fusion(f32[6,2304,128]{2,1,0:T(8,128)S(1)} %scatter-add.25, f32[4,2304,256]{2,1,0:T(8,128)} %copy-done.1, f32[4,256]{1,0:T(4,128)S(1)} %log_add_fusion, pred[4,2304]{1,0:T(4,128)(4,1)S(1)} %bitcast.256, bf16[128,4,256]{2,0,1:T(8,128)(2,1)S(1)} %fusion.56), kind=kOutput, calls=%fused_computation.50 | convolution fusion | flops 612237312 | bytes 19149824 | tf_op jit(solution)/shard_map/while/body/eval_jaxpr/cnm,cne->cme/dot_general | solution.py:151
  133.8 5.2 %fusion.34 = f32[1,1,6,2304,128]{4,3,2,1,0:T(8,128)} fusion(f32[1,1,6,2304,128]{4,3,2,1,0:T(8,128)} %copy.137, f32[6,2304,128]{2,1,0:T(8,128)S(1)} %fusion.27, f32[4,2304,256]{2,1,0:T(8,128)S(1)} %get-tuple-element.194, f32[4,256]{1,0:T(4,128)S(1)} %log_add_fusion, pred[4,2304]{1,0:T(4,128)(4,1)S(1)} %bitcast.251, bf16[128,4,256]{2,0,1:T(8,128)(2,1)S(1)} %fusion.56), kind=kOutput, calls=%fused_computation.60 | convolution fusion | flops 612237312 | bytes 19149824 | tf_op jit(solution)/shard_map/while/body/eval_jaxpr/cnm,cne->cme/dot_general | solution.py:151
  140.9 4.1 %fusion.30 = f32[6,2304,128]{2,1,0:T(8,128)S(1)} fusion(f32[6,2304,128]{2,1,0:T(8,128)S(1)} %scatter-add.20, bf16[4,256,2304]{1,2,0:T(8,128)(2,1)} %multiply_convert_fusion.1, bf16[1,1,1,4,256,128]{5,4,3,2,1,0:T(8,128)(2,1)S(1)} %copy-done.8), kind=kOutput, calls=%fused_computation.55 | convolution fusion | flops 606339072 | bytes 14417920 | tf_op jit(solution)/shard_map/while/body/eval_jaxpr/cnm,cne->cme/dot_general | solution.py:146
  147.9 3.6 %fusion.32 = f32[1,1,6,2304,128]{4,3,2,1,0:T(8,128)} fusion(f32[1,1,6,2304,128]{4,3,2,1,0:T(8,128)} %copy.139, bf16[4,256,2304]{1,2,0:T(8,128)(2,1)S(1)} %bitcast.223, f32[6,2304,128]{2,1,0:T(8,128)S(1)} %fusion.30, bf16[1,1,1,4,256,128]{5,4,3,2,1,0:T(8,128)(2,1)S(1)} %copy-done.8), kind=kOutput, calls=%fused_computation.58 | convolution fusion | flops 606339072 | bytes 14417920 | tf_op jit(solution)/shard_map/while/body/eval_jaxpr/cnm,cne->cme/dot_general | solution.py:146
  151.5 11.0 %pad_maximum_fusion = f32[2,1,6,2304,128]{4,3,2,1,0:T(8,128)} fusion(f32[1,1,6,2304,128]{4,3,2,1,0:T(8,128)} %fusion.34, f32[1,1,6,2304,128]{4,3,2,1,0:T(8,128)} %fusion.32), kind=kLoop, calls=%fused_computation.2 | loop fusion | flops 3538944 | bytes 28311552 | tf_op jit(solution)/shard_map/stack | solution.py:164
  162.5 6.7 %fusion.96 = bf16[2,1,3,3,4,256,128]{6,5,4,0,3,2,1:T(8,128)(2,1)} fusion(f32[2,1,6,3,3,256,128]{6,5,4,3,2,0,1:T(8,128)} %bitcast.216), kind=kLoop, calls=%fused_computation.125 | loop fusion | bytes 14155776 | tf_op jit(solution)/shard_map/convert.6
  173.2 3.9 %slice_bitcast_fusion.2 = (bf16[2,1,3,4,256,128]{5,4,3,0,2,1:T(8,128)(2,1)}, bf16[2,1,3,4,256,128]{5,4,3,0,2,1:T(8,128)(2,1)}) fusion(bf16[2,1,3,3,4,256,128]{6,5,4,0,3,2,1:T(8,128)(2,1)} %fusion.96), kind=kLoop, calls=%fused_computation.74 | loop fusion | bytes 6291456 | tf_op jit(solution)/shard_map/convert_element_type | solution.py:169
  179.0 5.1 %collective-permute-start.4 = (bf16[2,1,3,4,256,128]{5,4,3,0,2,1:T(8,128)(2,1)}, bf16[2,1,3,4,256,128]{5,4,3,0,2,1:T(8,128)(2,1)}, u32[]{:S(2)}, u32[]{:S(2)}) collective-permute-start(bf16[2,1,3,4,256,128]{5,4,3,0,2,1:T(8,128)(2,1)} %get-tuple-element.184), channel_id=1, source_target_pairs={{0,32},{32,64},{64,96},{1,33},{33,65},{65,97},{2,34},{34,66},{66,9... | collective-permute-start | bytes 4718600 | tf_op jit(solution)/shard_map/ppermute | solution.py:27
  185.4 3.6 %fusion.35 = bf16[1536,4,256]{0,2,1:T(8,128)(2,1)} fusion(bf16[4,256,128]{1,2,0:T(8,128)(2,1)} %get-tuple-element.200, bf16[1536,128]{1,0:T(8,128)(2,1)S(1)} %copy-done.15), kind=kOutput, calls=%fused_computation.62 | convolution fusion | flops 404226048 | bytes 3801088 | tf_op jit(solution)/shard_map/dhe,hcne->dcn/dot_general | solution.py:97
  189.0 5.9 %copy.76 = bf16[1536,4,256]{2,1,0:T(4,128)(2,1)} copy(bf16[1536,4,256]{0,2,1:T(8,128)(2,1)} %fusion.35) | data formatting | bytes 6291456 | tf_op jit(solution)/shard_map/convert_element_type | solution.py:99
  195.0 5.0 %fusion.102 = f32[4,256,128]{2,1,0:T(8,128)S(1)} fusion(bf16[4,256,2304]{1,2,0:T(8,128)(2,1)} %multiply_convert_fusion, bf16[4,2304,128]{2,1,0:T(8,128)(2,1)} %bitcast.229), kind=kOutput, calls=%fused_computation.130 | convolution fusion | flops 603979776 | bytes 7602176 | tf_op jit(solution)/shard_map/while/body/eval_jaxpr/cnm,cme->cne/dot_general | solution.py:139
  200.0 4.4 %copy_bitcast_fusion = f32[2,1,3,3,4,256,128]{6,5,4,0,3,2,1:T(8,128)S(1)} fusion(f32[2,1,6,3,3,256,128]{6,5,4,3,2,0,1:T(8,128)} %bitcast.217), kind=kLoop, calls=%fused_computation.4 | loop fusion | bytes 18874368 | tf_op jit(solution)/shard_map/transpose | solution.py:168
  204.4 4.7 %fusion.97 = (bf16[2,1,3,4,256,128]{5,4,3,0,2,1:T(8,128)(2,1)S(1)}, f32[2,1,3,4,256,128]{5,4,3,0,2,1:T(8,128)}) fusion(bf16[2,1,3,4,256,128]{5,4,3,0,2,1:T(8,128)(2,1)} %collective-permute-done.5, bf16[2,1,3,4,256,128]{5,4,3,0,2,1:T(8,128)(2,1)} %collective-permute-done.4, f32[2,1,3,3,4,256,128]{6,5,4,0,3,2,1:T(8,128)S(1)} %copy_bitcast_fusion), kind=kLoop, calls=%fused_computation.126 | loop fusion | flops 3932160 | bytes 11010048 | tf_op jit(solution)/shard_map/convert.4
  212.0 5.4 %collective-permute-start.6 = (bf16[2,1,4,256,128]{4,3,2,0,1:T(8,128)(2,1)}, bf16[2,1,4,256,128]{4,3,2,0,1:T(8,128)(2,1)}, u32[]{:S(2)}, u32[]{:S(2)}) collective-permute-start(bf16[2,1,4,256,128]{4,3,2,0,1:T(8,128)(2,1)} %get-tuple-element.186), channel_id=1, source_target_pairs={{0,8},{8,16},{16,24},{1,9},{9,17},{17,25},{2,10},{10,18},{18,26},{... | collective-permute-start | bytes 1572872 | tf_op jit(solution)/shard_map/ppermute | solution.py:27
  221.6 31.5 %reduce-scatter.4.cloned.1.call-done = bf16[96,128]{1,0:T(8,128)(2,1)} async-done(((bf16[1536,128]{1,0:T(8,128)(2,1)}), bf16[96,128]{1,0:T(8,128)(2,1)}) %reduce-scatter.4.cloned.1.call-update) | async-done | bytes 24592
  257.2 82.8 %all-reduce.7.cloned.1.call-done = bf16[1536,4,256]{2,1,0:T(4,128)(2,1)} async-done(((bf16[1536,4,256]{2,1,0:T(4,128)(2,1)}), bf16[1536,4,256]{2,1,0:T(4,128)(2,1)}) %all-reduce.7.cloned.1.call-update) | async-done | bytes 3145744
  (89 shorter events, 45.5 us)
Async XLA Ops:
  8.0 25.6 %copy-start = (bf16[1536,1,1,4,256]{4,3,2,1,0:T(4,128)(2,1)S(1)}, bf16[1536,1,1,4,256]{4,3,2,1,0:T(4,128)(2,1)}, u32[]{:S(2)}) copy-start(bf16[1536,1,1,4,256]{4,3,2,1,0:T(4,128)(2,1)} %param.23) | copy-start | bytes 9437188
  8.0 51.7 %copy-start.12 = (bf16[1,1,1,4,256,128]{5,4,3,2,1,0:T(8,128)(2,1)S(1)}, bf16[1,1,1,4,256,128]{5,4,3,2,1,0:T(8,128)(2,1)}, u32[]{:S(2)}) copy-start(bf16[1,1,1,4,256,128]{5,4,3,2,1,0:T(8,128)(2,1)} %param.20) | copy-start | bytes 786436
  8.0 245.0 %reduce-scatter.4.cloned.1.call-start = ((), (), s32[]{:S(2)}) async-start(), calls=%async_computation.1 | async-start | bytes 417792
  9.3 13.1 %collective-permute-start.1 = (bf16[2,1,1,1,4,256,128]{6,5,3,2,4,1,0:T(8,128)(2,1)S(1)}, bf16[2,1,1,1,4,256,128]{6,5,3,2,4,1,0:T(8,128)(2,1)S(1)}, u32[]{:S(2)}, u32[]{:S(2)}) collective-permute-start(bf16[2,1,1,1,4,256,128]{6,5,3,2,4,1,0:T(8,128)(2,1)S(1)} %pad_maximum_fusion.2), channel_id=1, source_target_pairs={{32,0},{64,32},{96,64},{33,1},{65,33},{97,65},{34,2},{66,34},{98,6... | collective-permute-start | bytes 1572872 | tf_op jit(solution)/shard_map/ppermute | solution.py:19
  12.6 10.9 %collective-permute-start = (bf16[2,1,1,1,4,256,128]{6,5,3,2,4,1,0:T(8,128)(2,1)S(1)}, bf16[2,1,1,1,4,256,128]{6,5,3,2,4,1,0:T(8,128)(2,1)S(1)}, u32[]{:S(2)}, u32[]{:S(2)}) collective-permute-start(bf16[2,1,1,1,4,256,128]{6,5,3,2,4,1,0:T(8,128)(2,1)S(1)} %pad_maximum_fusion.2), channel_id=1, source_target_pairs={{0,32},{32,64},{64,96},{1,33},{33,65},{65,97},{2,34},{34,66},{66,9... | collective-permute-start | bytes 1572872 | tf_op jit(solution)/shard_map/ppermute | solution.py:16
  26.1 31.8 %collective-permute-start.3 = (bf16[2,1,3,1,4,256,128]{6,5,3,2,4,1,0:T(8,128)(2,1)}, bf16[2,1,3,1,4,256,128]{6,5,3,2,4,1,0:T(8,128)(2,1)}, u32[]{:S(2)}, u32[]{:S(2)}) collective-permute-start(bf16[2,1,3,1,4,256,128]{6,5,3,2,4,1,0:T(8,128)(2,1)} %pad_maximum_fusion.1), channel_id=1, source_target_pairs={{8,0},{16,8},{24,16},{9,1},{17,9},{25,17},{10,2},{18,10},{26,18},{... | collective-permute-start | bytes 4718600 | tf_op jit(solution)/shard_map/ppermute | solution.py:19
  27.4 32.3 %collective-permute-start.2 = (bf16[2,1,3,1,4,256,128]{6,5,3,2,4,1,0:T(8,128)(2,1)}, bf16[2,1,3,1,4,256,128]{6,5,3,2,4,1,0:T(8,128)(2,1)}, u32[]{:S(2)}, u32[]{:S(2)}) collective-permute-start(bf16[2,1,3,1,4,256,128]{6,5,3,2,4,1,0:T(8,128)(2,1)} %pad_maximum_fusion.1), channel_id=1, source_target_pairs={{0,8},{8,16},{16,24},{1,9},{9,17},{17,25},{2,10},{10,18},{18,26},{... | collective-permute-start | bytes 4718600 | tf_op jit(solution)/shard_map/ppermute | solution.py:16
  64.6 3.2 copy-start.8
  67.8 9.8 %copy-start.5 = (bf16[1,1,4,3,3,256,128]{6,5,4,3,2,1,0:T(8,128)(2,1)}, bf16[1,1,4,3,3,256,128]{6,5,4,3,2,1,0:T(8,128)(2,1)S(1)}, u32[]{:S(2)}) copy-start(bf16[1,1,4,3,3,256,128]{6,5,4,3,2,1,0:T(8,128)(2,1)S(1)} %get-tuple-element.182) | copy-start | bytes 7077892
  67.8 9.8 %copy-start.7 = (bf16[1,1,4,3,3,256,128]{6,5,4,3,2,1,0:T(8,128)(2,1)}, bf16[1,1,4,3,3,256,128]{6,5,4,3,2,1,0:T(8,128)(2,1)S(1)}, u32[]{:S(2)}) copy-start(bf16[1,1,4,3,3,256,128]{6,5,4,3,2,1,0:T(8,128)(2,1)S(1)} %get-tuple-element.181) | copy-start | bytes 7077892
  67.9 9.9 %copy-start.3 = (bf16[1,1,4,3,3,256,128]{6,5,4,3,2,1,0:T(8,128)(2,1)}, bf16[1,1,4,3,3,256,128]{6,5,4,3,2,1,0:T(8,128)(2,1)S(1)}, u32[]{:S(2)}) copy-start(bf16[1,1,4,3,3,256,128]{6,5,4,3,2,1,0:T(8,128)(2,1)S(1)} %get-tuple-element.183) | copy-start | bytes 7077892
  77.7 7.0 %copy-start.1 = (f32[4,2304,256]{2,1,0:T(8,128)}, f32[4,2304,256]{2,1,0:T(8,128)S(1)}, u32[]{:S(2)}) copy-start(f32[4,2304,256]{2,1,0:T(8,128)S(1)} %get-tuple-element.196) | copy-start | bytes 28311556
  84.7 6.3 %copy-start.11 = (bf16[1,1,4,3,3,256,128]{6,5,4,3,2,1,0:T(8,128)(2,1)S(1)}, bf16[1,1,4,3,3,256,128]{6,5,4,3,2,1,0:T(8,128)(2,1)}, u32[]{:S(2)}) copy-start(bf16[1,1,4,3,3,256,128]{6,5,4,3,2,1,0:T(8,128)(2,1)} %get-tuple-element.179) | copy-start | bytes 7077892
  90.9 3.2 copy-start.10
  94.1 6.0 %copy-start.9 = (bf16[1,1,4,3,3,256,128]{6,5,4,3,2,1,0:T(8,128)(2,1)S(1)}, bf16[1,1,4,3,3,256,128]{6,5,4,3,2,1,0:T(8,128)(2,1)}, u32[]{:S(2)}) copy-start(bf16[1,1,4,3,3,256,128]{6,5,4,3,2,1,0:T(8,128)(2,1)} %get-tuple-element.178) | copy-start | bytes 7077892
  120.7 18.3 %copy-start.2 = (bf16[4,256,2304]{1,2,0:T(8,128)(2,1)}, bf16[4,256,2304]{1,2,0:T(8,128)(2,1)S(1)}, u32[]{:S(2)}) copy-start(bf16[4,256,2304]{1,2,0:T(8,128)(2,1)S(1)} %multiply_convert_fusion.2) | copy-start | bytes 14155780
  140.4 7.5 %slice-start.4 = ((s8[4718592]{0:T(1024)(128)(4,1)}), s8[4194304]{0:T(1024)(128)(4,1)S(1)}, s32[]{:S(2)}) async-start(s8[4718592]{0:T(1024)(128)(4,1)} %bitcast.222), calls=%async_computation.7 | async-start | bytes 8388608
  140.9 7.0 %slice-start.5 = ((s8[4718592]{0:T(1024)(128)(4,1)}), s8[524288]{0:T(1024)(128)(4,1)S(1)}, s32[]{:S(2)}) async-start(s8[4718592]{0:T(1024)(128)(4,1)} %bitcast.222), calls=%async_computation.8 | async-start | bytes 1048576
  162.5 6.7 %copy-start.16 = (bf16[4,256,128]{1,2,0:T(8,128)(2,1)S(1)}, bf16[4,256,128]{1,2,0:T(8,128)(2,1)}, u32[]{:S(2)}) copy-start(bf16[4,256,128]{1,2,0:T(8,128)(2,1)} %get-tuple-element.200) | copy-start | bytes 786436
  169.2 14.9 %copy-start.17 = (u32[128]{0:T(128)S(1)}, u32[128]{0:T(128)}, u32[]{:S(2)}) copy-start(u32[128]{0:T(128)} %constant.260) | copy-start | bytes 1540
  169.2 16.2 %copy-start.15 = (bf16[1536,128]{1,0:T(8,128)(2,1)S(1)}, bf16[1536,128]{1,0:T(8,128)(2,1)}, u32[]{:S(2)}) copy-start(bf16[1536,128]{1,0:T(8,128)(2,1)} %param.22) | copy-start | bytes 1179652
  173.1 166.9 %all-reduce.7.cloned.1.call-start = ((), (), s32[]{:S(2)}) async-start(), calls=%async_computation.2 | async-start | bytes 6291456
  177.1 27.3 %collective-permute-start.5 = (bf16[2,1,3,4,256,128]{5,4,3,0,2,1:T(8,128)(2,1)}, bf16[2,1,3,4,256,128]{5,4,3,0,2,1:T(8,128)(2,1)}, u32[]{:S(2)}, u32[]{:S(2)}) collective-permute-start(bf16[2,1,3,4,256,128]{5,4,3,0,2,1:T(8,128)(2,1)} %get-tuple-element.185), channel_id=1, source_target_pairs={{32,0},{64,32},{96,64},{33,1},{65,33},{97,65},{34,2},{66,34},{98,6... | collective-permute-start | bytes 4718600 | tf_op jit(solution)/shard_map/ppermute | solution.py:27
  179.0 25.4 %collective-permute-start.4 = (bf16[2,1,3,4,256,128]{5,4,3,0,2,1:T(8,128)(2,1)}, bf16[2,1,3,4,256,128]{5,4,3,0,2,1:T(8,128)(2,1)}, u32[]{:S(2)}, u32[]{:S(2)}) collective-permute-start(bf16[2,1,3,4,256,128]{5,4,3,0,2,1:T(8,128)(2,1)} %get-tuple-element.184), channel_id=1, source_target_pairs={{0,32},{32,64},{64,96},{1,33},{33,65},{65,97},{2,34},{34,66},{66,9... | collective-permute-start | bytes 4718600 | tf_op jit(solution)/shard_map/ppermute | solution.py:27
  195.0 22.4 %slice-start.2 = ((s8[4718592]{0:T(1024)(128)(4,1)}), s8[4194304]{0:T(1024)(128)(4,1)S(1)}, s32[]{:S(2)}) async-start(s8[4718592]{0:T(1024)(128)(4,1)} %bitcast.220), calls=%async_computation.5 | async-start | bytes 8388608
  200.0 17.5 %slice-start.3 = ((s8[4718592]{0:T(1024)(128)(4,1)}), s8[524288]{0:T(1024)(128)(4,1)S(1)}, s32[]{:S(2)}) async-start(s8[4718592]{0:T(1024)(128)(4,1)} %bitcast.220), calls=%async_computation.6 | async-start | bytes 1048576
  204.4 13.1 %copy-start.6 = (bf16[1,1,4,3,3,256,128]{6,5,4,3,2,1,0:T(8,128)(2,1)S(1)}, bf16[1,1,4,3,3,256,128]{6,5,4,3,2,1,0:T(8,128)(2,1)}, u32[]{:S(2)}) copy-start(bf16[1,1,4,3,3,256,128]{6,5,4,3,2,1,0:T(8,128)(2,1)} %copy-done.5) | copy-start | bytes 7077892
  209.1 10.2 %slice-start = ((s8[4718592]{0:T(1024)(128)(4,1)}), s8[4194304]{0:T(1024)(128)(4,1)S(1)}, s32[]{:S(2)}) async-start(s8[4718592]{0:T(1024)(128)(4,1)} %bitcast.218), calls=%async_computation.3 | async-start | bytes 8388608
  209.1 10.2 %copy-start.4 = (bf16[1,1,4,3,3,256,128]{6,5,4,3,2,1,0:T(8,128)(2,1)S(1)}, bf16[1,1,4,3,3,256,128]{6,5,4,3,2,1,0:T(8,128)(2,1)}, u32[]{:S(2)}) copy-start(bf16[1,1,4,3,3,256,128]{6,5,4,3,2,1,0:T(8,128)(2,1)} %copy-done.3) | copy-start | bytes 7077892
  210.2 44.4 %collective-permute-start.7 = (bf16[2,1,4,256,128]{4,3,2,1,0:T(8,128)(2,1)}, bf16[2,1,4,256,128]{4,3,2,1,0:T(8,128)(2,1)}, u32[]{:S(2)}, u32[]{:S(2)}) collective-permute-start(bf16[2,1,4,256,128]{4,3,2,1,0:T(8,128)(2,1)} %get-tuple-element.187), channel_id=1, source_target_pairs={{8,0},{16,8},{24,16},{9,1},{17,9},{25,17},{10,2},{18,10},{26,18},{... | collective-permute-start | bytes 1572872 | tf_op jit(solution)/shard_map/ppermute | solution.py:27
  212.0 7.3 %slice-start.1 = ((s8[4718592]{0:T(1024)(128)(4,1)}), s8[524288]{0:T(1024)(128)(4,1)S(1)}, s32[]{:S(2)}) async-start(s8[4718592]{0:T(1024)(128)(4,1)} %bitcast.218), calls=%async_computation.4 | async-start | bytes 1048576
  212.0 42.6 %collective-permute-start.6 = (bf16[2,1,4,256,128]{4,3,2,0,1:T(8,128)(2,1)}, bf16[2,1,4,256,128]{4,3,2,0,1:T(8,128)(2,1)}, u32[]{:S(2)}, u32[]{:S(2)}) collective-permute-start(bf16[2,1,4,256,128]{4,3,2,0,1:T(8,128)(2,1)} %get-tuple-element.186), channel_id=1, source_target_pairs={{0,8},{8,16},{16,24},{1,9},{9,17},{17,25},{2,10},{10,18},{18,26},{... | collective-permute-start | bytes 1572872 | tf_op jit(solution)/shard_map/ppermute | solution.py:27
  (2 other events, 3.8 us)
Sparse Core Ops, SparseCore 0:
  173.2 79.7 reduce-scatter.3
Sparse Core Ops, SparseCore 1:
  195.1 144.9 all-reduce.6
where the time goes:
time: 351 us; the launch traced here: 349 us
  waiting for transfers between devices  145 us (41%)
  matrix products  84.6 us (24%)
  local copies, waits for them, and re-layouts  38.9 us (11%)
  other arithmetic  35.1 us (10%)
  starting transfers between devices  29.1 us (8%)
  between operations  16.6 us (5%)
    unnamed x4, waiting for transfers between devices  114 us
    ppermute x2, waiting for transfers between devices, padded(): lax.ppermute(lax.slice_in_dim(block, 0, width, axis=dim), axis, backward)  27.7 us
    dot_general x3, matrix products, backward_head(): jnp.einsum('cne,cme->cnm', grad_head, value_cols[offset:offset + span_col...  16.8 us
    dot_general x3, matrix products, backward_head(): jnp.einsum('cnm,cne->cme', probs.astype(jnp.bfloat16), grad_head, preferr...  15 us
    dot_general x3, matrix products, block_scores(): jnp.einsum('cne,cme->cnm', query_head, key_part, preferred_element_type=j...  14.7 us
    ppermute x4, starting transfers between devices, passed_along(): return lax.ppermute(value, axis, pairs)  14.3 us
    dot_general x3, matrix products, forward_head(): jnp.einsum('cnm,cme->cne', weights, value_cols[offset:offset + span_cols]...  12.9 us
    unnamed x55, local copies, waits for them, and re-layouts  11.8 us
  transfers between devices with their start and end apart: 10, of which 6 were waited for; matrix products, arithmetic and copies ran while one was open for 11% of the time, Pallas kernels for 0%

commit v1 on v0

v1 whole, which is shorter than its diff:
```python
import functools
import math

import jax
import jax.numpy as jnp
from jax import lax
from jax.experimental import pallas as pl
from jax.experimental.pallas import tpu as pltpu
from jax.sharding import PartitionSpec as P

MESH = pl.DeviceIdType.MESH
F32 = jnp.float32
BF16 = jnp.bfloat16

TILE = 256
SPAN = 4
TOKENS = TILE * SPAN
HD = 128
D = 1536
HEADS = 8
NT = 4
NH = 4
GROUP = NT * NH
SCALE = 1.0 / math.sqrt(HD)
EXPO = SCALE * math.log2(math.e)
LOWEST = -1e30

SLOTS = 9
BACK_ORDER = (7, 8, 5, 6, 3, 4, 2, 1, 0)

PAIRS = [(k, q) for k in range(SPAN) for q in range(SPAN) if abs(k - q) <= 1]
PAIR_AT = {pair: i for i, pair in enumerate(PAIRS)}


def dot(lhs, rhs, dims=((1,), (0,))):
    return lax.dot_general(lhs, rhs, (dims, ((), ())), preferred_element_type=F32)


def chosen(index, table):
    value = jnp.int32(table[0])
    for at, entry in enumerate(table):
        value = jnp.where(index == at, jnp.int32(entry), value)
    return value


def kernel(
    q_ref, k_ref, v_ref, tv_ref, w_ref, og_ref,
    mixed_ref, dq_ref, dk_ref, dv_ref, wg_ref,
    q_s, kv_s, kt_s, vt_s, mask_s, w_s, og_s,
    qt_s, do_s, dot_s, p_s, ps_s, ds_s, att_s, m_s, mb_s, rl_s, dqt_s,
    acc_s, send_s, rp_s, rz_s, rx_s, ry_s, ag_s, wgat_s, prod_s, red_s,
    loc_sem, f_send, f_recv, b_send, b_recv, ag_send, ag_recv, wt_send, wt_recv, pr_send, pr_recv,
):
    a = lax.axis_index("tm")
    b = lax.axis_index("height")
    h = lax.axis_index("head")
    inner = jnp.logical_or(a == 1, a == 2)
    has_lo = b > 0
    has_hi = b < NH - 1
    partner = a + 1 - 2 * (a % 2)
    cross = NT - 1 - a
    here = a * NH + b
    dev_partner = (partner, b, h)
    dev_cross = (cross, b, h)
    dev_lo = (a, b - 1, h)
    dev_hi = (a, b + 1, h)
    both = jnp.logical_and

    loads = [
        pltpu.make_async_copy(src, dst, loc_sem.at[i])
        for i, (src, dst) in enumerate(
            [(q_ref, q_s), (k_ref, kv_s.at[0, 0]), (v_ref, kv_s.at[0, 1]), (w_ref, w_s), (og_ref, og_s)]
        )
    ]
    for load in loads:
        load.start()

    barrier = pltpu.get_barrier_semaphore()
    for j in range(1, GROUP):
        peer = (here + j) % GROUP
        pl.semaphore_signal(barrier, inc=1, device_id=(peer // NH, peer % NH, h), device_id_type=MESH)
    for j in range(1, HEADS):
        pl.semaphore_signal(barrier, inc=1, device_id=(a, b, (h + j) % HEADS), device_id_type=MESH)
    pl.semaphore_wait(barrier, GROUP - 1 + HEADS - 1)

    def remote(src, dst, send, recv, device):
        return pltpu.make_async_remote_copy(
            src_ref=src, dst_ref=dst, send_sem=send, recv_sem=recv, device_id=device, device_id_type=MESH
        )

    yes = a >= 0
    hops = [
        (-1, 3, dev_hi, has_hi),
        (-1, 4, dev_lo, has_lo),
        (-1, 2, dev_cross, inner),
        (-1, 1, dev_partner, yes),
        (3, 5, dev_partner, has_lo),
        (4, 6, dev_partner, has_hi),
        (2, 7, dev_hi, both(inner, has_hi)),
        (2, 8, dev_lo, both(inner, has_lo)),
    ]
    arrives = [yes, yes, inner, has_lo, has_hi, has_lo, has_hi, both(inner, has_lo), both(inner, has_hi)]

    def hop_copies(n):
        source, target, device, _ = hops[n]
        return [
            remote(
                (k_ref, v_ref)[i] if source < 0 else kv_s.at[source, i],
                kv_s.at[target, i], f_send.at[n, i], f_recv.at[target, i], device,
            )
            for i in range(2)
        ]

    def start_hop(n):
        @pl.when(hops[n][3])
        def _():
            for copy in hop_copies(n):
                copy.start()

    def wait_slot(slot):
        @pl.when(arrives[slot])
        def _():
            for i in range(2):
                remote(
                    k_ref, kv_s.at[slot, i], f_send.at[0, 0], f_recv.at[slot, i], dev_partner
                ).wait_recv()

    for n in range(4):
        start_hop(n)

    share = D // HEADS

    def weight_copy(j):
        peer = (h + j) % HEADS
        return remote(
            w_ref.at[pl.ds(pl.multiple_of(peer * share, share), share)], wgat_s.at[h],
            wt_send.at[j], wt_recv.at[j], (a, b, peer),
        )

    for j in range(1, HEADS):
        weight_copy(j).start()

    for load in loads[:3]:
        load.wait()
    first_row = (lax.broadcasted_iota(jnp.int32, (HD, TILE), 0) == 0).astype(BF16)
    for c in range(SPAN):
        rows = slice(c * TILE, (c + 1) * TILE)
        qt_s[c, :HD] = q_s[rows].T
        qt_s[c, HD:] = first_row
        m_s[c] = jnp.full((1, TILE), LOWEST, F32)
        att_s[c] = jnp.zeros((HD + 16, TILE), F32)
    ones_rows = jnp.ones((16, TOKENS), BF16)
    ones_cols = jnp.ones((TILE, HD), BF16)

    def span_of(c):
        return max(0, c - 1), min(SPAN, c + 2)

    def place(slot):
        frame = chosen(slot, (0, 1, 2, 0, 0, 1, 1, 2, 2))
        frame = jnp.where(frame == 0, a, jnp.where(frame == 1, partner, cross))
        row = b + chosen(slot, (0, 0, 0, -1, 1, -1, 1, -1, 1))
        return frame, row

    def exists(slot):
        far = chosen(slot, (0, 0, 1, 0, 0, 0, 0, 1, 1))
        row = b + chosen(slot, (0, 0, 0, -1, 1, -1, 1, -1, 1))
        near = both(row >= 0, row < NH)
        return both(near, jnp.logical_or(far == 0, inner))

    def forward_column(slot):
        frame, row = place(slot)
        for c in range(SPAN):
            rows = slice(c * TILE, (c + 1) * TILE)
            kt_s[slot, :, rows] = kv_s[slot, 0, rows].T
            vt_s[slot, :, rows] = kv_s[slot, 1, rows].T
            valid = tv_ref[pl.ds((frame * NH + row) * SPAN + c, 1), :]
            bias = jnp.where(valid > 0, 0.0, LOWEST)
            mask_s[rows] = jnp.broadcast_to(bias, (HD, TILE)).T.astype(BF16)
        for c in range(SPAN):
            lo, hi = span_of(c)
            rows = slice(lo * TILE, hi * TILE)
            keys = jnp.concatenate([kv_s[slot, 0, rows], mask_s[rows]], axis=1)
            scores = dot(keys, qt_s[c])
            old = m_s[c]
            new = jnp.maximum(old, jnp.max(scores, axis=0, keepdims=True))
            weights = jnp.exp2((scores - new) * EXPO).astype(BF16)
            for t in range(lo, hi):
                p_s[slot, PAIR_AT[t, c]] = weights[(t - lo) * TILE:(t - lo + 1) * TILE]
            vals = jnp.concatenate([vt_s[slot, :, rows], ones_rows[:, rows]], axis=0)
            att_s[c] = att_s[c] * jnp.exp2((old - new) * EXPO) + dot(vals, weights)
            m_s[c] = new
            mb_s[slot, c] = new

    def grad_attended():
        for load in loads[3:]:
            load.wait()
        for c in range(SPAN):
            rows = slice(c * TILE, (c + 1) * TILE)
            grad = dot(w_s[...], og_s[:, rows], ((0,), (0,))).astype(BF16)
            dot_s[c, :HD] = grad
            do_s[rows] = grad.T

    def forward_step(i, carry):
        @pl.when(i == 1)
        def _():
            grad_attended()
            wait_slot(1)

        @pl.when(i == 2)
        def _():
            wait_slot(2)
            start_hop(6)
            start_hop(7)

        @pl.when(i == 3)
        def _():
            wait_slot(3)
            start_hop(4)
            wait_slot(4)
            start_hop(5)

        for slot in range(5, SLOTS):
            @pl.when(i == slot)
            def _():
                wait_slot(slot)

        @pl.when(exists(i))
        def _():
            forward_column(i)

        return carry

    lax.fori_loop(0, SLOTS, forward_step, 0)

    for c in range(SPAN):
        rows = slice(c * TILE, (c + 1) * TILE)
        inverse = 1.0 / att_s[c, HD:HD + 1]
        rl_s[c] = inverse
        attended = (att_s[c, :HD] * inverse).astype(BF16)
        ag_s[h, :, rows] = attended
        delta = jnp.sum(dot_s[c, :HD].astype(F32) * attended.astype(F32), axis=0, keepdims=True)
        high = delta.astype(BF16).astype(F32)
        middle = (delta - high).astype(BF16).astype(F32)
        low = delta - high - middle
        index = lax.broadcasted_iota(jnp.int32, (HD, TILE), 0)
        extra = jnp.where(index == 0, -high, jnp.where(index == 1, -middle, jnp.where(index == 2, -low, 0.0)))
        dot_s[c, HD:] = extra.astype(BF16)
        dqt_s[c] = jnp.zeros((HD, TILE), F32)

    def gather_copy(j):
        return remote(ag_s.at[h], ag_s.at[h], ag_send.at[j], ag_recv.at[j], (a, b, (h + j) % HEADS))

    for j in range(1, HEADS):
        gather_copy(j).start()

    part = D // GROUP

    def part_copy(j):
        peer = (here + j) % GROUP
        return remote(
            prod_s.at[peer], red_s.at[here], pr_send.at[j], pr_recv.at[j], (peer // NH, peer % NH, h)
        )

    for n in range(GROUP):
        prod_s[n] = dot(og_s[n * part:(n + 1) * part], ag_s[h], ((1,), (1,))).astype(BF16)
    for j in range(1, GROUP):
        part_copy(j).start()

    def backward_column(slot):
        factors = [
            jnp.exp2((mb_s[slot, c] - m_s[c]) * EXPO) * rl_s[c] for c in range(SPAN)
        ]
        for t in range(SPAN):
            rows = slice(t * TILE, (t + 1) * TILE)
            lo, hi = span_of(t)
            vals = jnp.concatenate([kv_s[slot, 1, rows], ones_cols], axis=1)
            for c in range(lo, hi):
                n = PAIR_AT[t, c]
                grad = dot(vals, dot_s[c])
                probs = p_s[slot, n].astype(F32) * factors[c]
                ps_s[n] = probs.astype(BF16)
                ds_s[n] = (probs * grad).astype(BF16)
            near = slice(lo * TILE, hi * TILE)
            many_ds = jnp.concatenate([ds_s[PAIR_AT[t, c]] for c in range(lo, hi)], axis=1)
            many_ps = jnp.concatenate([ps_s[PAIR_AT[t, c]] for c in range(lo, hi)], axis=1)
            acc_s[0, rows] = dot(many_ds, q_s[near]) * SCALE
            acc_s[1, rows] = dot(many_ps, do_s[near])
        for c in range(SPAN):
            lo, hi = span_of(c)
            many = jnp.concatenate([ds_s[PAIR_AT[t, c]] for t in range(lo, hi)], axis=0)
            dqt_s[c] += dot(kt_s[slot, :, lo * TILE:hi * TILE], many)

    back = {
        7: (rx_s.at[0], 0, dev_lo, both(inner, has_lo)),
        8: (rx_s.at[1], 1, dev_hi, both(inner, has_hi)),
        5: (rp_s.at[1], 2, dev_partner, has_lo),
        6: (rp_s.at[2], 3, dev_partner, has_hi),
        3: (rz_s.at[0], 4, dev_lo, has_lo),
        4: (rz_s.at[1], 5, dev_hi, has_hi),
        2: (ry_s, 6, dev_cross, inner),
        1: (rp_s.at[0], 7, dev_partner, yes),
    }
    back_arrives = {
        7: both(inner, has_hi), 8: both(inner, has_lo), 5: has_lo, 6: has_hi,
        3: has_hi, 4: has_lo, 2: inner, 1: yes,
    }

    def back_copy(slot):
        target, index, device, _ = back[slot]
        return remote(send_s.at[slot - 1], target, b_send.at[slot - 1], b_recv.at[index], device)

    def add_arrived(slot):
        @pl.when(back_arrives[slot])
        def _():
            back_copy(slot).wait_recv()
            acc_s[...] += back[slot][0][...].astype(F32)

    needs = {7: (), 8: (), 5: (), 6: (), 3: (5,), 4: (6,), 2: (7, 8), 1: ()}

    def backward_step(i, carry):
        slot = chosen(i, BACK_ORDER)

        @pl.when(exists(slot))
        def _():
            backward_column(slot)

        for n in range(1, SLOTS):
            @pl.when(both(slot == n, back[n][3]))
            def _():
                for source in needs[n]:
                    add_arrived(source)
                send_s[n - 1] = acc_s[...].astype(BF16)
                back_copy(n).start()

        return carry

    lax.fori_loop(0, SLOTS, backward_step, 0)

    for c in range(SPAN):
        rows = slice(c * TILE, (c + 1) * TILE)
        dq_ref[rows] = (dqt_s[c] * SCALE).T.astype(BF16)

    loads_w = w_s[pl.ds(pl.multiple_of(h * share, share), share)]
    wgat_s[h] = loads_w
    for j in range(1, HEADS):
        weight_copy(j).wait_recv()
        gather_copy(j).wait_recv()
    weights = jnp.concatenate([wgat_s[n] for n in range(HEADS)], axis=1)
    for c in range(SPAN):
        rows = slice(c * TILE, (c + 1) * TILE)
        everyone = jnp.concatenate([ag_s[n, :, rows] for n in range(HEADS)], axis=0)
        mixed_ref[:, rows] = dot(weights, everyone).astype(BF16)

    red_s[here] = prod_s[here]
    for j in range(1, GROUP):
        part_copy(j).wait_recv()
    total = red_s[0].astype(F32)
    for n in range(1, GROUP):
        total = total + red_s[n].astype(F32)
    wg_ref[...] = total

    for slot in (1, 4, 3, 2):
        add_arrived(slot)
    dk_ref[...] = acc_s[0].astype(BF16)
    dv_ref[...] = acc_s[1].astype(BF16)

    for n in range(len(hops)):
        @pl.when(hops[n][3])
        def _():
            for copy in hop_copies(n):
                copy.wait_send()
    for slot in range(1, SLOTS):
        @pl.when(back[slot][3])
        def _():
            back_copy(slot).wait_send()
    for j in range(1, HEADS):
        weight_copy(j).wait_send()
        gather_copy(j).wait_send()
    for j in range(1, GROUP):
        part_copy(j).wait_send()


def per_device(queries, key_tiles, values, token_valid, out_weight, out_grad):
    any_spec = pl.BlockSpec(memory_space=pl.ANY)
    vmem_spec = pl.BlockSpec(memory_space=pltpu.VMEM)
    vmem = pltpu.VMEM
    dma = pltpu.SemaphoreType.DMA
    token = jax.ShapeDtypeStruct((TOKENS, HD), BF16)
    pair = (2, TOKENS, HD)
    mixed, dq, dk, dv, wg = pl.pallas_call(
        kernel,
        out_shape=(
            jax.ShapeDtypeStruct((D // HEADS, TOKENS), BF16),
            token, token, token,
            jax.ShapeDtypeStruct((D // GROUP, HD), F32),
        ),
        in_specs=[any_spec, any_spec, any_spec, vmem_spec, any_spec, any_spec],
        out_specs=(vmem_spec,) * 5,
        scratch_shapes=[
            vmem((TOKENS, HD), BF16),
            vmem((SLOTS,) + pair, BF16),
            vmem((SLOTS, HD, TOKENS), BF16),
            vmem((SLOTS, HD, TOKENS), BF16),
            vmem((TOKENS, HD), BF16),
            vmem((D, HD), BF16),
            vmem((D, TOKENS), BF16),
            vmem((SPAN, 2 * HD, TILE), BF16),
            vmem((TOKENS, HD), BF16),
            vmem((SPAN, 2 * HD, TILE), BF16),
            vmem((SLOTS, len(PAIRS), TILE, TILE), BF16),
            vmem((len(PAIRS), TILE, TILE), BF16),
            vmem((len(PAIRS), TILE, TILE), BF16),
            vmem((SPAN, HD + 16, TILE), F32),
            vmem((SPAN, 1, TILE), F32),
            vmem((SLOTS, SPAN, 1, TILE), F32),
            vmem((SPAN, 1, TILE), F32),
            vmem((SPAN, HD, TILE), F32),
            vmem(pair, F32),
            vmem((SLOTS - 1,) + pair, BF16),
            vmem((3,) + pair, BF16),
            vmem((2,) + pair, BF16),
            vmem((2,) + pair, BF16),
            vmem(pair, BF16),
            vmem((HEADS, HD, TOKENS), BF16),
            vmem((HEADS, D // HEADS, HD), BF16),
            vmem((GROUP, D // GROUP, HD), BF16),
            vmem((GROUP, D // GROUP, HD), BF16),
            dma((5,)), dma((8, 2)), dma((SLOTS, 2)), dma((SLOTS - 1,)), dma((SLOTS - 1,)),
            dma((HEADS,)), dma((HEADS,)), dma((HEADS,)), dma((HEADS,)), dma((GROUP,)), dma((GROUP,)),
        ],
        compiler_params=pltpu.CompilerParams(
            collective_id=0, has_side_effects=True, vmem_limit_bytes=60 * 1024 * 1024
        ),
    )(
        queries.reshape(TOKENS, HD),
        key_tiles.reshape(TOKENS, HD),
        values.reshape(TOKENS, HD),
        token_valid.reshape(GROUP * SPAN, TILE),
        out_weight,
        out_grad.reshape(D, TOKENS),
    )
    tile_shape = (1, 1, 1, SPAN, TILE, HD)
    return (
        mixed.reshape(D // HEADS, 1, 1, SPAN, TILE),
        dq.reshape(tile_shape),
        dk.reshape(tile_shape),
        dv.reshape(tile_shape),
        wg,
    )


def solution(mesh):
    placed = (
        P("head", "tm", "height", None, None, None),
        P("head", "tm", "height", None, None, None),
        P("head", "tm", "height", None, None, None),
        P(),
        P(None, "head"),
        P(None, "tm", "height", None, None),
    )
    return jax.shard_map(
        per_device,
        mesh=mesh,
        in_specs=placed,
        out_specs=(
            P("head", "tm", "height", None, None),
            P("head", "tm", "height", None, None, None),
            P("head", "tm", "height", None, None, None),
            P("head", "tm", "height", None, None, None),
            P(("tm", "height"), "head"),
        ),
        check_vma=False,
    )
```

time: 351 us -> 82 us (0.23)
  the two profiles are of different devices: /device:TPU:1 before, /device:TPU:48 now
where the time goes in v1:
time: 82 us; the launch traced here: 81.5 us
  Pallas kernels  66.6 us (81%)
  local copies, waits for them, and re-layouts  14.3 us (17%)
    pallas_call x1, Pallas kernels, per_device(): pl.pallas_call(kernel, out_shape=(jax.ShapeDtypeStruct((D // HEADS, TOKEN...  66.6 us
    unnamed x5, local copies, waits for them, and re-layouts  10.7 us
    reshape x1, local copies, waits for them, and re-layouts, per_device(): mixed.reshape(D // HEADS, 1, 1, SPAN, TILE)  2.03 us

profile of v1, /device:TPU:48, one launch (start us, length us, event | category | flops | bytes accessed | tf_op | source)
XLA Modules:
  0.0 81.5 jit_solution(16520994638968010743)
XLA Ops:
  0.6 1.5 %reshape.40.tv_ref = s32[64,256]{1,0:T(8,128)} reshape(s32[4,4,4,256]{3,2,1,0:T(4,128)} %param.9) | data formatting | bytes 131072 | tf_op jit(solution)/shard_map/reshape | solution.py:438
  2.1 4.3 %copy.12 = bf16[192,8,4,256]{3,1,2,0:T(8,128)(2,1)} copy(bf16[192,8,4,256]{3,2,1,0:T(4,128)(2,1)} %bitcast.11) | data formatting | bytes 6291456
  6.4 66.6 %shard_map.101 = (bf16[192,1024]{1,0:T(8,128)(2,1)}, bf16[1024,128]{1,0:T(8,128)(2,1)}, bf16[1024,128]{1,0:T(8,128)(2,1)}, bf16[1024,128]{1,0:T(8,128)(2,1)}, f32[96,128]{1,0:T(8,128)}) custom-call(bf16[1024,128]{1,0:T(8,128)(2,1)} %bitcast.13, bf16[1024,128]{1,0:T(8,128)(2,1)} %bitcast.14, bf16[1024,128]{1,0:T(8,128)(2,1)} %bitcast.15, ...), custom_call_target="tpu_custom_call" | custom-call | tf_op jit(solution)/shard_map/pallas_call | solution.py:390
  73.1 2.0 %reshape.42 = bf16[192,1,1,4,256]{4,3,0,2,1:T(4,128)(2,1)} reshape(bf16[192,1024]{1,0:T(8,128)(2,1)} %get-tuple-element.10) | data formatting | bytes 786432 | tf_op jit(solution)/shard_map/reshape | solution.py:444
  75.1 1.7 %copy.17 = bf16[1,1,1,4,256,128]{5,4,3,2,1,0:T(8,128)(2,1)} copy(bf16[1,1,1,4,256,128]{5,4,3,2,1,0:T(8,128)(2,1)} %bitcast.18) | data formatting | bytes 524288
  76.8 1.7 %copy.18 = bf16[1,1,1,4,256,128]{5,4,3,2,1,0:T(8,128)(2,1)} copy(bf16[1,1,1,4,256,128]{5,4,3,2,1,0:T(8,128)(2,1)} %bitcast.17) | data formatting | bytes 524288
  78.4 1.7 %copy.19 = bf16[1,1,1,4,256,128]{5,4,3,2,1,0:T(8,128)(2,1)} copy(bf16[1,1,1,4,256,128]{5,4,3,2,1,0:T(8,128)(2,1)} %bitcast.16) | data formatting | bytes 524288
  80.1 1.4 %copy.20 = f32[96,128]{1,0:T(8,128)} copy(f32[96,128]{1,0:T(8,128)} %get-tuple-element.29) | data formatting | bytes 98304

commit v2 on v1

--- a/solution.py
+++ b/solution.py
@@ -46,7 +46,7 @@
 def kernel(
     q_ref, k_ref, v_ref, tv_ref, w_ref, og_ref,
     mixed_ref, dq_ref, dk_ref, dv_ref, wg_ref,
-    q_s, kv_s, kt_s, vt_s, mask_s, w_s, og_s,
+    q_s, kv_s, kt_s, vt_s, mask_s, w_s, raw_s, og_s,
     qt_s, do_s, dot_s, p_s, ps_s, ds_s, att_s, m_s, mb_s, rl_s, dqt_s,
     acc_s, send_s, rp_s, rz_s, rx_s, ry_s, ag_s, wgat_s, prod_s, red_s,
     loc_sem, f_send, f_recv, b_send, b_recv, ag_send, ag_recv, wt_send, wt_recv, pr_send, pr_recv,
@@ -69,7 +69,7 @@
     loads = [
         pltpu.make_async_copy(src, dst, loc_sem.at[i])
         for i, (src, dst) in enumerate(
-            [(q_ref, q_s), (k_ref, kv_s.at[0, 0]), (v_ref, kv_s.at[0, 1]), (w_ref, w_s), (og_ref, og_s)]
+            [(q_ref, q_s), (k_ref, kv_s.at[0, 0]), (v_ref, kv_s.at[0, 1]), (w_ref, w_s), (og_ref, raw_s)]
         )
     ]
     for load in loads:
@@ -173,7 +173,7 @@
             rows = slice(c * TILE, (c + 1) * TILE)
             kt_s[slot, :, rows] = kv_s[slot, 0, rows].T
             vt_s[slot, :, rows] = kv_s[slot, 1, rows].T
-            valid = tv_ref[pl.ds((frame * NH + row) * SPAN + c, 1), :]
+            valid = tv_ref[frame, row, c:c + 1, :]
             bias = jnp.where(valid > 0, 0.0, LOWEST)
             mask_s[rows] = jnp.broadcast_to(bias, (HD, TILE)).T.astype(BF16)
         for c in range(SPAN):
@@ -194,6 +194,8 @@
     def grad_attended():
         for load in loads[3:]:
             load.wait()
+        for n in range(0, D, HD):
+            og_s[n:n + HD] = raw_s[n:n + HD].reshape(HD, TOKENS)
         for c in range(SPAN):
             rows = slice(c * TILE, (c + 1) * TILE)
             grad = dot(w_s[...], og_s[:, rows], ((0,), (0,))).astype(BF16)
@@ -247,11 +249,34 @@
         dot_s[c, HD:] = extra.astype(BF16)
         dqt_s[c] = jnp.zeros((HD, TILE), F32)
 
-    def gather_copy(j):
-        return remote(ag_s.at[h], ag_s.at[h], ag_send.at[j], ag_recv.at[j], (a, b, (h + j) % HEADS))
-
-    for j in range(1, HEADS):
-        gather_copy(j).start()
+    side = h + 1 - 2 * (h % 2)
+    up, down = (h + 2) % HEADS, (h + HEADS - 2) % HEADS
+    side_up, side_down = (side + 2) % HEADS, (side + HEADS - 2) % HEADS
+    half = HD // 2
+    low_half, high_half = pl.ds(0, half), pl.ds(half, half)
+    gathers = [
+        (ag_s.at[h], side),
+        (ag_s.at[h], up),
+        (ag_s.at[h], down),
+        (ag_s.at[side], up),
+        (ag_s.at[side], down),
+        (ag_s.at[down, low_half], up),
+        (ag_s.at[up, high_half], down),
+        (ag_s.at[side_down, low_half], up),
+        (ag_s.at[side_up, high_half], down),
+    ]
+
+    def gather_copy(n):
+        block, peer = gathers[n]
+        return remote(block, block, ag_send.at[n], ag_recv.at[n], (a, b, peer))
+
+    def relay(waits, starts):
+        for n in waits:
+            gather_copy(n).wait_recv()
+        for n in starts:
+            gather_copy(n).start()
+
+    relay((), (0, 1, 2))
 
     part = D // GROUP
 
@@ -320,6 +345,15 @@
     def backward_step(i, carry):
         slot = chosen(i, BACK_ORDER)
 
+        @pl.when(i == 4)
+        def _():
+            relay((0,), (3, 4))
+            relay((1, 2), (5, 6))
+
+        @pl.when(i == 7)
+        def _():
+            relay((3, 4), (7, 8))
+
         @pl.when(exists(slot))
         def _():
             backward_column(slot)
@@ -344,12 +378,10 @@
     wgat_s[h] = loads_w
     for j in range(1, HEADS):
         weight_copy(j).wait_recv()
-        gather_copy(j).wait_recv()
+    relay((5, 6, 7, 8), ())
     weights = jnp.concatenate([wgat_s[n] for n in range(HEADS)], axis=1)
-    for c in range(SPAN):
-        rows = slice(c * TILE, (c + 1) * TILE)
-        everyone = jnp.concatenate([ag_s[n, :, rows] for n in range(HEADS)], axis=0)
-        mixed_ref[:, rows] = dot(weights, everyone).astype(BF16)
+    everyone = jnp.concatenate([ag_s[n] for n in range(HEADS)], axis=0)
+    mixed_ref[...] = dot(weights, everyone).astype(BF16).reshape(share, SPAN, TILE)
 
     red_s[here] = prod_s[here]
     for j in range(1, GROUP):
@@ -375,9 +407,23 @@
             back_copy(slot).wait_send()
     for j in range(1, HEADS):
         weight_copy(j).wait_send()
-        gather_copy(j).wait_send()
+    for n in range(len(gathers)):
+        gather_copy(n).wait_send()
     for j in range(1, GROUP):
         part_copy(j).wait_send()
+
+
+def hand_over(*refs):
+    sources, targets, staged, sem = refs[:5], refs[5:10], refs[10:15], refs[15]
+    reads = [pltpu.make_async_copy(sources[i], staged[i], sem.at[i]) for i in range(5)]
+    writes = [pltpu.make_async_copy(staged[i], targets[i], sem.at[i + 5]) for i in range(5)]
+    for read in reads:
+        read.start()
+    for read, write in zip(reads, writes):
+        read.wait()
+        write.start()
+    for write in writes:
+        write.wait()
 
 
 def per_device(queries, key_tiles, values, token_valid, out_weight, out_grad):
@@ -387,10 +433,10 @@
     dma = pltpu.SemaphoreType.DMA
     token = jax.ShapeDtypeStruct((TOKENS, HD), BF16)
     pair = (2, TOKENS, HD)
-    mixed, dq, dk, dv, wg = pl.pallas_call(
+    results = pl.pallas_call(
         kernel,
         out_shape=(
-            jax.ShapeDtypeStruct((D // HEADS, TOKENS), BF16),
+            jax.ShapeDtypeStruct((D // HEADS, SPAN, TILE), BF16),
             token, token, token,
             jax.ShapeDtypeStruct((D // GROUP, HD), F32),
         ),
@@ -403,6 +449,7 @@
             vmem((SLOTS, HD, TOKENS), BF16),
             vmem((TOKENS, HD), BF16),
             vmem((D, HD), BF16),
+            vmem((D, SPAN, TILE), BF16),
             vmem((D, TOKENS), BF16),
             vmem((SPAN, 2 * HD, TILE), BF16),
             vmem((TOKENS, HD), BF16),
@@ -426,7 +473,7 @@
             vmem((GROUP, D // GROUP, HD), BF16),
             vmem((GROUP, D // GROUP, HD), BF16),
             dma((5,)), dma((8, 2)), dma((SLOTS, 2)), dma((SLOTS - 1,)), dma((SLOTS - 1,)),
-            dma((HEADS,)), dma((HEADS,)), dma((HEADS,)), dma((HEADS,)), dma((GROUP,)), dma((GROUP,)),
+            dma((9,)), dma((9,)), dma((HEADS,)), dma((HEADS,)), dma((GROUP,)), dma((GROUP,)),
         ],
         compiler_params=pltpu.CompilerParams(
             collective_id=0, has_side_effects=True, vmem_limit_bytes=60 * 1024 * 1024
@@ -435,10 +482,17 @@
         queries.reshape(TOKENS, HD),
         key_tiles.reshape(TOKENS, HD),
         values.reshape(TOKENS, HD),
-        token_valid.reshape(GROUP * SPAN, TILE),
+        token_valid,
         out_weight,
-        out_grad.reshape(D, TOKENS),
+        out_grad.reshape(D, SPAN, TILE),
     )
+    mixed, dq, dk, dv, wg = pl.pallas_call(
+        hand_over,
+        out_shape=[jax.ShapeDtypeStruct(r.shape, r.dtype) for r in results],
+        in_specs=[any_spec] * 5,
+        out_specs=[any_spec] * 5,
+        scratch_shapes=[vmem(r.shape, r.dtype) for r in results] + [dma((10,))],
+    )(*results)
     tile_shape = (1, 1, 1, SPAN, TILE, HD)
     return (
         mixed.reshape(D // HEADS, 1, 1, SPAN, TILE),

time: 82 us -> 64.9 us (0.79)
  the two profiles are of different devices: /device:TPU:48 before, /device:TPU:1 now
where the time goes in v2:
time: 64.9 us; the launch traced here: 64.8 us
  Pallas kernels  64.1 us (99%)
    pallas_call x1, Pallas kernels, per_device(): pl.pallas_call(kernel, out_shape=(jax.ShapeDtypeStruct((D // HEADS, SPAN,...  62 us
    pallas_call x1, Pallas kernels, per_device(): pl.pallas_call(hand_over, out_shape=[jax.ShapeDtypeStruct(r.shape, r.dtyp...  2.09 us

profile of v2, /device:TPU:1, one launch (start us, length us, event | category | flops | bytes accessed | tf_op | source)
XLA Modules:
  0.0 64.8 jit_solution(12013343378427417405)
XLA Ops:
  0.6 62.0 %shard_map.101 = (bf16[192,4,256]{2,1,0:T(4,128)(2,1)}, bf16[1024,128]{1,0:T(8,128)(2,1)}, bf16[1024,128]{1,0:T(8,128)(2,1)}, bf16[1024,128]{1,0:T(8,128)(2,1)}, f32[96,128]{1,0:T(8,128)}) custom-call(bf16[1024,128]{1,0:T(8,128)(2,1)} %bitcast.11, bf16[1024,128]{1,0:T(8,128)(2,1)} %bitcast.12, bf16[1024,128]{1,0:T(8,128)(2,1)} %bitcast.13, ...), custom_call_target="tpu_custom_call" | custom-call | tf_op jit(solution)/shard_map/pallas_call | solution.py:436
  62.7 2.1 %shard_map.102 = (bf16[192,4,256]{2,1,0:T(4,128)(2,1)}, bf16[1024,128]{1,0:T(8,128)(2,1)}, bf16[1024,128]{1,0:T(8,128)(2,1)}, bf16[1024,128]{1,0:T(8,128)(2,1)}, f32[96,128]{1,0:T(8,128)}) custom-call(bf16[192,4,256]{2,1,0:T(4,128)(2,1)} %get-tuple-element.15.refs_0_, bf16[1024,128]{1,0:T(8,128)(2,1)} %get-tuple-element.16.refs_1_, ...), custom_call_target="tpu_custom_call" | custom-call | tf_op jit(solution)/shard_map/pallas_call | solution.py:489

commit v3 on v2

--- a/solution.py
+++ b/solution.py
@@ -26,7 +26,8 @@
 LOWEST = -1e30
 
 SLOTS = 9
-BACK_ORDER = (7, 8, 5, 6, 3, 4, 2, 1, 0)
+HALF = TOKENS // 2
+BACK_ORDER = (7, 8, 5, 6, 2, 3, 4, 1, 0)
 
 PAIRS = [(k, q) for k in range(SPAN) for q in range(SPAN) if abs(k - q) <= 1]
 PAIR_AT = {pair: i for i, pair in enumerate(PAIRS)}
@@ -48,7 +49,7 @@
     mixed_ref, dq_ref, dk_ref, dv_ref, wg_ref,
     q_s, kv_s, kt_s, vt_s, mask_s, w_s, raw_s, og_s,
     qt_s, do_s, dot_s, p_s, ps_s, ds_s, att_s, m_s, mb_s, rl_s, dqt_s,
-    acc_s, send_s, rp_s, rz_s, rx_s, ry_s, ag_s, wgat_s, prod_s, red_s,
+    acc_s, send_s, rp_s, rz_s, rx_s, rd_s, ry_s, ag_s, wgat_s, prod_s, pair_s, sum_s, red_s,
     loc_sem, f_send, f_recv, b_send, b_recv, ag_send, ag_recv, wt_send, wt_recv, pr_send, pr_recv,
 ):
     a = lax.axis_index("tm")
@@ -69,11 +70,15 @@
     loads = [
         pltpu.make_async_copy(src, dst, loc_sem.at[i])
         for i, (src, dst) in enumerate(
-            [(q_ref, q_s), (k_ref, kv_s.at[0, 0]), (v_ref, kv_s.at[0, 1]), (w_ref, w_s), (og_ref, raw_s)]
+            [(q_ref, q_s), (w_ref, w_s), (og_ref, raw_s)]
+            + [
+                (ref.at[pl.ds(part * HALF, HALF)], kv_s.at[0, part, kind])
+                for part in range(2) for kind, ref in enumerate((k_ref, v_ref))
+            ]
         )
     ]
-    for load in loads:
-        load.start()
+    for n in (3, 4, 5, 6, 0, 1, 2):
+        loads[n].start()
 
     barrier = pltpu.get_barrier_semaphore()
     for j in range(1, GROUP):
@@ -90,43 +95,42 @@
 
     yes = a >= 0
     hops = [
-        (-1, 3, dev_hi, has_hi),
-        (-1, 4, dev_lo, has_lo),
-        (-1, 2, dev_cross, inner),
-        (-1, 1, dev_partner, yes),
-        (3, 5, dev_partner, has_lo),
-        (4, 6, dev_partner, has_hi),
-        (2, 7, dev_hi, both(inner, has_hi)),
-        (2, 8, dev_lo, both(inner, has_lo)),
+        (0, 3, dev_hi, has_hi, (0, 1)),
+        (0, 4, dev_lo, has_lo, (0, 1)),
+        (0, 2, dev_cross, inner, (0, 1)),
+        (0, 1, dev_partner, yes, (0, 1)),
+        (3, 5, dev_partner, has_lo, (0, 1)),
+        (4, 6, dev_partner, has_hi, (0, 1)),
+        (2, 7, dev_hi, both(inner, has_hi), (1,)),
+        (2, 8, dev_lo, both(inner, has_lo), (1,)),
+        (3, 7, dev_cross, both(inner, has_lo), (0,)),
+        (4, 8, dev_cross, both(inner, has_hi), (0,)),
     ]
     arrives = [yes, yes, inner, has_lo, has_hi, has_lo, has_hi, both(inner, has_lo), both(inner, has_hi)]
 
-    def hop_copies(n):
-        source, target, device, _ = hops[n]
-        return [
+    def hop_copy(n, part):
+        source, target, device, _, _ = hops[n]
+        return remote(
+            kv_s.at[source, part], kv_s.at[target, part], f_send.at[n, part], f_recv.at[target, part], device
+        )
+
+    def start_hop(n, part):
+        @pl.when(hops[n][3])
+        def _():
+            hop_copy(n, part).start()
+
+    def wait_unit(slot, part):
+        @pl.when(arrives[slot])
+        def _():
             remote(
-                (k_ref, v_ref)[i] if source < 0 else kv_s.at[source, i],
-                kv_s.at[target, i], f_send.at[n, i], f_recv.at[target, i], device,
-            )
-            for i in range(2)
-        ]
-
-    def start_hop(n):
-        @pl.when(hops[n][3])
-        def _():
-            for copy in hop_copies(n):
-                copy.start()
-
-    def wait_slot(slot):
-        @pl.when(arrives[slot])
-        def _():
-            for i in range(2):
-                remote(
-                    k_ref, kv_s.at[slot, i], f_send.at[0, 0], f_recv.at[slot, i], dev_partner
-                ).wait_recv()
-
-    for n in range(4):
-        start_hop(n)
+                kv_s.at[slot, part], kv_s.at[slot, part], f_send.at[0, 0], f_recv.at[slot, part], dev_partner
+            ).wait_recv()
+
+    for n in range(3, 7):
+        loads[n].wait()
+    for part in range(2):
+        for n in range(4):
+            start_hop(n, part)
 
     share = D // HEADS
 
@@ -140,8 +144,7 @@
     for j in range(1, HEADS):
         weight_copy(j).start()
 
-    for load in loads[:3]:
-        load.wait()
+    loads[0].wait()
     first_row = (lax.broadcasted_iota(jnp.int32, (HD, TILE), 0) == 0).astype(BF16)
     for c in range(SPAN):
         rows = slice(c * TILE, (c + 1) * TILE)
@@ -152,8 +155,18 @@
     ones_rows = jnp.ones((16, TOKENS), BF16)
     ones_cols = jnp.ones((TILE, HD), BF16)
 
-    def span_of(c):
-        return max(0, c - 1), min(SPAN, c + 2)
+    def keys_of(c, tiles):
+        near = [t for t in tiles if abs(t - c) <= 1]
+        return (near[0], near[-1] + 1) if near else (0, 0)
+
+    def tile_of(ref, slot, kind, t):
+        return ref[slot, t // 2, kind, (t % 2) * TILE:(t % 2 + 1) * TILE]
+
+    def queries_of(t):
+        return max(0, t - 1), min(SPAN, t + 2)
+
+    def near_queries(tiles):
+        return [c for c in range(SPAN) if keys_of(c, tiles)[1]]
 
     def place(slot):
         frame = chosen(slot, (0, 1, 2, 0, 0, 1, 1, 2, 2))
@@ -167,32 +180,39 @@
         near = both(row >= 0, row < NH)
         return both(near, jnp.logical_or(far == 0, inner))
 
-    def forward_column(slot):
+    def forward_unit(slot, tiles):
         frame, row = place(slot)
-        for c in range(SPAN):
-            rows = slice(c * TILE, (c + 1) * TILE)
-            kt_s[slot, :, rows] = kv_s[slot, 0, rows].T
-            vt_s[slot, :, rows] = kv_s[slot, 1, rows].T
-            valid = tv_ref[frame, row, c:c + 1, :]
+        for t in tiles:
+            rows = slice(t * TILE, (t + 1) * TILE)
+            kt_s[slot, :, rows] = tile_of(kv_s, slot, 0, t).T
+            vt_s[slot, :, rows] = tile_of(kv_s, slot, 1, t).T
+            valid = tv_ref[frame, row, t:t + 1, :]
             bias = jnp.where(valid > 0, 0.0, LOWEST)
             mask_s[rows] = jnp.broadcast_to(bias, (HD, TILE)).T.astype(BF16)
-        for c in range(SPAN):
-            lo, hi = span_of(c)
-            rows = slice(lo * TILE, hi * TILE)
-            keys = jnp.concatenate([kv_s[slot, 0, rows], mask_s[rows]], axis=1)
+        shrink = {}
+        for c in near_queries(tiles):
+            lo, hi = keys_of(c, tiles)
+            keys = jnp.concatenate([tile_of(kv_s, slot, 0, t) for t in range(lo, hi)], axis=0)
+            keys = jnp.concatenate([keys, mask_s[lo * TILE:hi * TILE]], axis=1)
             scores = dot(keys, qt_s[c])
             old = m_s[c]
             new = jnp.maximum(old, jnp.max(scores, axis=0, keepdims=True))
             weights = jnp.exp2((scores - new) * EXPO).astype(BF16)
             for t in range(lo, hi):
                 p_s[slot, PAIR_AT[t, c]] = weights[(t - lo) * TILE:(t - lo + 1) * TILE]
+            shrink[c] = jnp.exp2((old - new) * EXPO)
+            m_s[c] = new
+            for part in sorted({t // 2 for t in range(lo, hi)}):
+                mb_s[slot, part, c] = new
+        for c in near_queries(tiles):
+            lo, hi = keys_of(c, tiles)
+            rows = slice(lo * TILE, hi * TILE)
             vals = jnp.concatenate([vt_s[slot, :, rows], ones_rows[:, rows]], axis=0)
-            att_s[c] = att_s[c] * jnp.exp2((old - new) * EXPO) + dot(vals, weights)
-            m_s[c] = new
-            mb_s[slot, c] = new
+            weights = jnp.concatenate([p_s[slot, PAIR_AT[t, c]] for t in range(lo, hi)], axis=0)
+            att_s[c] = att_s[c] * shrink[c] + dot(vals, weights)
 
     def grad_attended():
-        for load in loads[3:]:
+        for load in loads[1:3]:
             load.wait()
         for n in range(0, D, HD):
             og_s[n:n + HD] = raw_s[n:n + HD].reshape(HD, TOKENS)
@@ -202,37 +222,35 @@
             dot_s[c, :HD] = grad
             do_s[rows] = grad.T
 
-    def forward_step(i, carry):
-        @pl.when(i == 1)
-        def _():
-            grad_attended()
-            wait_slot(1)
-
-        @pl.when(i == 2)
-        def _():
-            wait_slot(2)
-            start_hop(6)
-            start_hop(7)
-
-        @pl.when(i == 3)
-        def _():
-            wait_slot(3)
-            start_hop(4)
-            wait_slot(4)
-            start_hop(5)
-
-        for slot in range(5, SLOTS):
-            @pl.when(i == slot)
+    every = tuple(range(SPAN))
+
+    def forward_pass(first, count, tiles, events):
+        def step(i, carry):
+            for at, waits in events.items():
+                @pl.when(i == at - first)
+                def _():
+                    if at == 1:
+                        grad_attended()
+                    for source, part, starts in waits:
+                        wait_unit(source, part)
+                        for n in starts:
+                            start_hop(n, part)
+
+            @pl.when(exists(i + first))
             def _():
-                wait_slot(slot)
-
-        @pl.when(exists(i))
-        def _():
-            forward_column(i)
-
-        return carry
-
-    lax.fori_loop(0, SLOTS, forward_step, 0)
+                forward_unit(i + first, tiles)
+
+            return carry
+
+        lax.fori_loop(0, count, step, 0)
+
+    forward_pass(0, 3, every, {
+        1: [(1, 0, ()), (1, 1, ())],
+        2: [(3, 0, (4, 8)), (4, 0, (5, 9)), (2, 0, ()), (2, 1, (6, 7))],
+    })
+    forward_pass(3, 4, (0, 1), {5: [(5, 0, ())], 6: [(6, 0, ())]})
+    forward_pass(3, 4, (2, 3), {3: [(3, 1, (4,)), (4, 1, (5,))], 5: [(5, 1, ())], 6: [(6, 1, ())]})
+    forward_pass(7, 2, every, {7: [(7, 0, ()), (7, 1, ())], 8: [(8, 0, ()), (8, 1, ())]})
 
     for c in range(SPAN):
         rows = slice(c * TILE, (c + 1) * TILE)
@@ -278,69 +296,90 @@
 
     relay((), (0, 1, 2))
 
-    part = D // GROUP
+    piece = D // GROUP
+    core = a % 2
+    chips = GROUP // 2
+    chip = (a // 2) * NH + b
+
+    def pair_copy():
+        return remote(prod_s.at[1 - core], pair_s, pr_send.at[0], pr_recv.at[0], dev_partner)
 
     def part_copy(j):
-        peer = (here + j) % GROUP
+        peer = (chip + j) % chips
         return remote(
-            prod_s.at[peer], red_s.at[here], pr_send.at[j], pr_recv.at[j], (peer // NH, peer % NH, h)
+            sum_s.at[peer], red_s.at[chip], pr_send.at[j], pr_recv.at[j], ((peer // NH) * 2 + core, peer % NH, h)
         )
 
-    for n in range(GROUP):
-        prod_s[n] = dot(og_s[n * part:(n + 1) * part], ag_s[h], ((1,), (1,))).astype(BF16)
-    for j in range(1, GROUP):
-        part_copy(j).start()
-
-    def backward_column(slot):
-        factors = [
-            jnp.exp2((mb_s[slot, c] - m_s[c]) * EXPO) * rl_s[c] for c in range(SPAN)
-        ]
-        for t in range(SPAN):
-            rows = slice(t * TILE, (t + 1) * TILE)
-            lo, hi = span_of(t)
-            vals = jnp.concatenate([kv_s[slot, 1, rows], ones_cols], axis=1)
-            for c in range(lo, hi):
+    def weight_product():
+        for n in range(GROUP):
+            frame, row = n // NH, n % NH
+            value = dot(og_s[n * piece:(n + 1) * piece], ag_s[h], ((1,), (1,)))
+            prod_s[frame % 2, (frame // 2) * NH + row] = value.astype(BF16)
+        pair_copy().start()
+
+    def weight_parts():
+        pair_copy().wait_recv()
+        sum_s[...] = (prod_s[core].astype(F32) + pair_s[...].astype(F32)).astype(BF16)
+        for j in range(1, chips):
+            part_copy(j).start()
+
+    def backward_unit(slot):
+        factors = {
+            (part, c): jnp.exp2((mb_s[slot, part, c] - m_s[c]) * EXPO) * rl_s[c]
+            for part in range(2) for c in near_queries((2 * part, 2 * part + 1))
+        }
+        for t in every:
+            vals = jnp.concatenate([tile_of(kv_s, slot, 1, t), ones_cols], axis=1)
+            for c in range(*queries_of(t)):
                 n = PAIR_AT[t, c]
                 grad = dot(vals, dot_s[c])
-                probs = p_s[slot, n].astype(F32) * factors[c]
+                probs = p_s[slot, n].astype(F32) * factors[t // 2, c]
                 ps_s[n] = probs.astype(BF16)
                 ds_s[n] = (probs * grad).astype(BF16)
+        for t in every:
+            rows = slice((t % 2) * TILE, (t % 2 + 1) * TILE)
+            lo, hi = queries_of(t)
             near = slice(lo * TILE, hi * TILE)
             many_ds = jnp.concatenate([ds_s[PAIR_AT[t, c]] for c in range(lo, hi)], axis=1)
             many_ps = jnp.concatenate([ps_s[PAIR_AT[t, c]] for c in range(lo, hi)], axis=1)
-            acc_s[0, rows] = dot(many_ds, q_s[near]) * SCALE
-            acc_s[1, rows] = dot(many_ps, do_s[near])
+            send_s[slot, t // 2, 0, rows] = (dot(many_ds, q_s[near]) * SCALE).astype(BF16)
+            send_s[slot, t // 2, 1, rows] = dot(many_ps, do_s[near]).astype(BF16)
         for c in range(SPAN):
-            lo, hi = span_of(c)
+            lo, hi = keys_of(c, every)
             many = jnp.concatenate([ds_s[PAIR_AT[t, c]] for t in range(lo, hi)], axis=0)
             dqt_s[c] += dot(kt_s[slot, :, lo * TILE:hi * TILE], many)
 
     back = {
-        7: (rx_s.at[0], 0, dev_lo, both(inner, has_lo)),
-        8: (rx_s.at[1], 1, dev_hi, both(inner, has_hi)),
-        5: (rp_s.at[1], 2, dev_partner, has_lo),
-        6: (rp_s.at[2], 3, dev_partner, has_hi),
-        3: (rz_s.at[0], 4, dev_lo, has_lo),
-        4: (rz_s.at[1], 5, dev_hi, has_hi),
-        2: (ry_s, 6, dev_cross, inner),
-        1: (rp_s.at[0], 7, dev_partner, yes),
+        (7, 0): (rd_s.at[0], 0, dev_cross, both(inner, has_lo), both(inner, has_lo)),
+        (8, 0): (rd_s.at[1], 1, dev_cross, both(inner, has_hi), both(inner, has_hi)),
+        (7, 1): (rx_s.at[0], 2, dev_lo, both(inner, has_lo), both(inner, has_hi)),
+        (8, 1): (rx_s.at[1], 3, dev_hi, both(inner, has_hi), both(inner, has_lo)),
     }
-    back_arrives = {
-        7: both(inner, has_hi), 8: both(inner, has_lo), 5: has_lo, 6: has_hi,
-        3: has_hi, 4: has_lo, 2: inner, 1: yes,
-    }
-
-    def back_copy(slot):
-        target, index, device, _ = back[slot]
-        return remote(send_s.at[slot - 1], target, b_send.at[slot - 1], b_recv.at[index], device)
-
-    def add_arrived(slot):
-        @pl.when(back_arrives[slot])
-        def _():
-            back_copy(slot).wait_recv()
-            acc_s[...] += back[slot][0][...].astype(F32)
-
-    needs = {7: (), 8: (), 5: (), 6: (), 3: (5,), 4: (6,), 2: (7, 8), 1: ()}
+    for part in range(2):
+        at = 4 + 6 * part
+        back[5, part] = (rp_s.at[1, part], at, dev_partner, has_lo, has_lo)
+        back[6, part] = (rp_s.at[2, part], at + 1, dev_partner, has_hi, has_hi)
+        back[3, part] = (rz_s.at[0, part], at + 2, dev_lo, has_lo, has_hi)
+        back[4, part] = (rz_s.at[1, part], at + 3, dev_hi, has_hi, has_lo)
+        back[2, part] = (ry_s.at[part], at + 4, dev_cross, inner, inner)
+        back[1, part] = (rp_s.at[0, part], at + 5, dev_partner, yes, yes)
+    needs = {key: () for key in back}
+    needs[3, 0], needs[4, 0] = ((5, 0), (7, 0)), ((6, 0), (8, 0))
+    needs[3, 1], needs[4, 1] = ((5, 1),), ((6, 1),)
+    needs[2, 1] = ((7, 1), (8, 1))
+
+    def back_copy(key):
+        slot, part = key
+        target, index, device, _, _ = back[key]
+        return remote(send_s.at[slot, part], target, b_send.at[index], b_recv.at[index], device)
+
+    def merge(key, source):
+        @pl.when(back[source][4])
+        def _():
+            back_copy(source).wait_recv()
+            slot, part = key
+            arrived = back[source][0][...].astype(F32)
+            send_s[slot, part] = (send_s[slot, part].astype(F32) + arrived).astype(BF16)
 
     def backward_step(i, carry):
         slot = chosen(i, BACK_ORDER)
@@ -349,6 +388,11 @@
         def _():
             relay((0,), (3, 4))
             relay((1, 2), (5, 6))
+            weight_product()
+
+        @pl.when(i == 6)
+        def _():
+            weight_parts()
 
         @pl.when(i == 7)
         def _():
@@ -356,15 +400,17 @@
 
         @pl.when(exists(slot))
         def _():
-            backward_column(slot)
+            backward_unit(slot)
 
         for n in range(1, SLOTS):
-            @pl.when(both(slot == n, back[n][3]))
+            @pl.when(slot == n)
             def _():
-                for source in needs[n]:
-                    add_arrived(source)
-                send_s[n - 1] = acc_s[...].astype(BF16)
-                back_copy(n).start()
+                for part in range(2):
+                    @pl.when(back[n, part][3])
+                    def _():
+                        for source in needs[n, part]:
+                            merge((n, part), source)
+                        back_copy((n, part)).start()
 
         return carry
 
@@ -383,33 +429,42 @@
     everyone = jnp.concatenate([ag_s[n] for n in range(HEADS)], axis=0)
     mixed_ref[...] = dot(weights, everyone).astype(BF16).reshape(share, SPAN, TILE)
 
-    red_s[here] = prod_s[here]
-    for j in range(1, GROUP):
+    red_s[chip] = sum_s[chip]
+    for j in range(1, chips):
         part_copy(j).wait_recv()
     total = red_s[0].astype(F32)
-    for n in range(1, GROUP):
+    for n in range(1, chips):
         total = total + red_s[n].astype(F32)
     wg_ref[...] = total
 
-    for slot in (1, 4, 3, 2):
-        add_arrived(slot)
-    dk_ref[...] = acc_s[0].astype(BF16)
-    dv_ref[...] = acc_s[1].astype(BF16)
+    for part in range(2):
+        back_copy((1, part)).wait_recv()
+        acc_s[part] = send_s[0, part].astype(F32) + rp_s[0, part].astype(F32)
+    for part in range(2):
+        for source in (4, 3, 2):
+            @pl.when(back[source, part][4])
+            def _():
+                back_copy((source, part)).wait_recv()
+                acc_s[part] += back[source, part][0][...].astype(F32)
+        rows = slice(part * HALF, (part + 1) * HALF)
+        dk_ref[rows] = acc_s[part, 0].astype(BF16)
+        dv_ref[rows] = acc_s[part, 1].astype(BF16)
 
     for n in range(len(hops)):
         @pl.when(hops[n][3])
         def _():
-            for copy in hop_copies(n):
-                copy.wait_send()
-    for slot in range(1, SLOTS):
-        @pl.when(back[slot][3])
-        def _():
-            back_copy(slot).wait_send()
+            for part in hops[n][4]:
+                hop_copy(n, part).wait_send()
+    for key, (_, _, _, sends, _) in back.items():
+        @pl.when(sends)
+        def _():
+            back_copy(key).wait_send()
     for j in range(1, HEADS):
         weight_copy(j).wait_send()
     for n in range(len(gathers)):
         gather_copy(n).wait_send()
-    for j in range(1, GROUP):
+    pair_copy().wait_send()
+    for j in range(1, chips):
         part_copy(j).wait_send()
 
 
@@ -432,7 +487,8 @@
     vmem = pltpu.VMEM
     dma = pltpu.SemaphoreType.DMA
     token = jax.ShapeDtypeStruct((TOKENS, HD), BF16)
-    pair = (2, TOKENS, HD)
+    unit = (2, HALF, HD)
+    pieces = (GROUP // 2, D // GROUP, HD)
     results = pl.pallas_call(
         kernel,
         out_shape=(
@@ -444,7 +500,7 @@
         out_specs=(vmem_spec,) * 5,
         scratch_shapes=[
             vmem((TOKENS, HD), BF16),
-            vmem((SLOTS,) + pair, BF16),
+            vmem((SLOTS, 2) + unit, BF16),
             vmem((SLOTS, HD, TOKENS), BF16),
             vmem((SLOTS, HD, TOKENS), BF16),
             vmem((TOKENS, HD), BF16),
@@ -459,21 +515,24 @@
             vmem((len(PAIRS), TILE, TILE), BF16),
             vmem((SPAN, HD + 16, TILE), F32),
             vmem((SPAN, 1, TILE), F32),
-            vmem((SLOTS, SPAN, 1, TILE), F32),
+            vmem((SLOTS, 2, SPAN, 1, TILE), F32),
             vmem((SPAN, 1, TILE), F32),
             vmem((SPAN, HD, TILE), F32),
-            vmem(pair, F32),
-            vmem((SLOTS - 1,) + pair, BF16),
-            vmem((3,) + pair, BF16),
-            vmem((2,) + pair, BF16),
-            vmem((2,) + pair, BF16),
-            vmem(pair, BF16),
+            vmem((2,) + unit, F32),
+            vmem((SLOTS, 2) + unit, BF16),
+            vmem((3, 2) + unit, BF16),
+            vmem((2, 2) + unit, BF16),
+            vmem((2,) + unit, BF16),
+            vmem((2,) + unit, BF16),
+            vmem((2,) + unit, BF16),
             vmem((HEADS, HD, TOKENS), BF16),
             vmem((HEADS, D // HEADS, HD), BF16),
-            vmem((GROUP, D // GROUP, HD), BF16),
-            vmem((GROUP, D // GROUP, HD), BF16),
-            dma((5,)), dma((8, 2)), dma((SLOTS, 2)), dma((SLOTS - 1,)), dma((SLOTS - 1,)),
-            dma((9,)), dma((9,)), dma((HEADS,)), dma((HEADS,)), dma((GROUP,)), dma((GROUP,)),
+            vmem((2,) + pieces, BF16),
+            vmem(pieces, BF16),
+            vmem(pieces, BF16),
+            vmem(pieces, BF16),
+            dma((7,)), dma((10, 2)), dma((SLOTS, 2)), dma((16,)), dma((16,)),
+            dma((9,)), dma((9,)), dma((HEADS,)), dma((HEADS,)), dma((GROUP // 2,)), dma((GROUP // 2,)),
         ],
         compiler_params=pltpu.CompilerParams(
             collective_id=0, has_side_effects=True, vmem_limit_bytes=60 * 1024 * 1024

time: 64.9 us -> 59.2 us (0.912)
  Pallas kernels: 64.1 us -> 57.8 us
    pallas_call x1, Pallas kernels: 62 us -> 55.7 us  [per_device(): pl.pallas_call(kernel, out_shape=(jax.ShapeDtypeStruct((D // HEADS, SPAN,...]
where the time goes in v3:
time: 59.2 us; the launch traced here: 58.4 us
  Pallas kernels  57.8 us (98%)
  between operations  0.64 us (1%)
    pallas_call x1, Pallas kernels, per_device(): pl.pallas_call(kernel, out_shape=(jax.ShapeDtypeStruct((D // HEADS, SPAN,...  55.7 us
    pallas_call x1, Pallas kernels, per_device(): pl.pallas_call(hand_over, out_shape=[jax.ShapeDtypeStruct(r.shape, r.dtyp...  2.09 us

profile of v3, /device:TPU:1, one launch (start us, length us, event | category | flops | bytes accessed | tf_op | source)
XLA Modules:
  0.0 58.4 jit_solution(18180284438556604460)
XLA Ops:
  0.6 55.7 %shard_map.101 = (bf16[192,4,256]{2,1,0:T(4,128)(2,1)}, bf16[1024,128]{1,0:T(8,128)(2,1)}, bf16[1024,128]{1,0:T(8,128)(2,1)}, bf16[1024,128]{1,0:T(8,128)(2,1)}, f32[96,128]{1,0:T(8,128)}) custom-call(bf16[1024,128]{1,0:T(8,128)(2,1)} %bitcast.11, bf16[1024,128]{1,0:T(8,128)(2,1)} %bitcast.12, bf16[1024,128]{1,0:T(8,128)(2,1)} %bitcast.13, ...), custom_call_target="tpu_custom_call" | custom-call | tf_op jit(solution)/shard_map/pallas_call | solution.py:492
  56.3 2.1 %shard_map.102 = (bf16[192,4,256]{2,1,0:T(4,128)(2,1)}, bf16[1024,128]{1,0:T(8,128)(2,1)}, bf16[1024,128]{1,0:T(8,128)(2,1)}, bf16[1024,128]{1,0:T(8,128)(2,1)}, f32[96,128]{1,0:T(8,128)}) custom-call(bf16[192,4,256]{2,1,0:T(4,128)(2,1)} %get-tuple-element.15.refs_0_, bf16[1024,128]{1,0:T(8,128)(2,1)} %get-tuple-element.16.refs_1_, ...), custom_call_target="tpu_custom_call" | custom-call | tf_op jit(solution)/shard_map/pallas_call | solution.py:548

commit v4 on v3

--- a/solution.py
+++ b/solution.py
@@ -27,7 +27,7 @@
 
 SLOTS = 9
 HALF = TOKENS // 2
-BACK_ORDER = (7, 8, 5, 6, 2, 3, 4, 1, 0)
+LAST_ORDER = (2, 3, 4, 1, 0)
 
 PAIRS = [(k, q) for k in range(SPAN) for q in range(SPAN) if abs(k - q) <= 1]
 PAIR_AT = {pair: i for i, pair in enumerate(PAIRS)}
@@ -47,10 +47,11 @@
 def kernel(
     q_ref, k_ref, v_ref, tv_ref, w_ref, og_ref,
     mixed_ref, dq_ref, dk_ref, dv_ref, wg_ref,
+    mixed_s, most_s, dq_s, dk_s, dv_s, wg_s, tv_s,
     q_s, kv_s, kt_s, vt_s, mask_s, w_s, raw_s, og_s,
     qt_s, do_s, dot_s, p_s, ps_s, ds_s, att_s, m_s, mb_s, rl_s, dqt_s,
-    acc_s, send_s, rp_s, rz_s, rx_s, rd_s, ry_s, ag_s, wgat_s, prod_s, pair_s, sum_s, red_s,
-    loc_sem, f_send, f_recv, b_send, b_recv, ag_send, ag_recv, wt_send, wt_recv, pr_send, pr_recv,
+    acc_s, send_s, rp_s, rz_s, rx_s, rd_s, rw_s, ry_s, ag_s, wgat_s, prod_s, pair_s, sum_s, red_s,
+    loc_sem, out_sem, f_send, f_recv, b_send, b_recv, ag_send, ag_recv, wt_send, wt_recv, pr_send, pr_recv,
 ):
     a = lax.axis_index("tm")
     b = lax.axis_index("height")
@@ -75,9 +76,10 @@
                 (ref.at[pl.ds(part * HALF, HALF)], kv_s.at[0, part, kind])
                 for part in range(2) for kind, ref in enumerate((k_ref, v_ref))
             ]
+            + [(tv_ref, tv_s)]
         )
     ]
-    for n in (3, 4, 5, 6, 0, 1, 2):
+    for n in (3, 4, 5, 6, 0, 7, 1, 2):
         loads[n].start()
 
     barrier = pltpu.get_barrier_semaphore()
@@ -134,17 +136,26 @@
 
     share = D // HEADS
 
+    part_share = share // 2
+    core = a % 2
+
+    def weight_rows(peer):
+        return pl.ds(pl.multiple_of(peer * share + core * part_share, part_share), part_share)
+
     def weight_copy(j):
         peer = (h + j) % HEADS
         return remote(
-            w_ref.at[pl.ds(pl.multiple_of(peer * share, share), share)], wgat_s.at[h],
-            wt_send.at[j], wt_recv.at[j], (a, b, peer),
+            w_ref.at[weight_rows(peer)], wgat_s.at[core, h], wt_send.at[j], wt_recv.at[j], (a, b, peer)
         )
+
+    def weight_exchange():
+        return remote(wgat_s.at[core], wgat_s.at[core], wt_send.at[0], wt_recv.at[0], dev_partner)
 
     for j in range(1, HEADS):
         weight_copy(j).start()
 
     loads[0].wait()
+    loads[7].wait()
     first_row = (lax.broadcasted_iota(jnp.int32, (HD, TILE), 0) == 0).astype(BF16)
     for c in range(SPAN):
         rows = slice(c * TILE, (c + 1) * TILE)
@@ -186,7 +197,7 @@
             rows = slice(t * TILE, (t + 1) * TILE)
             kt_s[slot, :, rows] = tile_of(kv_s, slot, 0, t).T
             vt_s[slot, :, rows] = tile_of(kv_s, slot, 1, t).T
-            valid = tv_ref[frame, row, t:t + 1, :]
+            valid = tv_s[frame, row, t:t + 1, :]
             bias = jnp.where(valid > 0, 0.0, LOWEST)
             mask_s[rows] = jnp.broadcast_to(bias, (HD, TILE)).T.astype(BF16)
         shrink = {}
@@ -244,12 +255,14 @@
 
         lax.fori_loop(0, count, step, 0)
 
-    forward_pass(0, 3, every, {
-        1: [(1, 0, ()), (1, 1, ())],
-        2: [(3, 0, (4, 8)), (4, 0, (5, 9)), (2, 0, ()), (2, 1, (6, 7))],
+    forward_pass(0, 2, every, {1: [(1, 0, ()), (1, 1, ())]})
+    forward_pass(2, 5, (0, 1), {
+        2: [(2, 0, ())],
+        3: [(3, 0, (4, 8)), (4, 0, (5, 9))],
+        5: [(2, 1, (6, 7)), (5, 0, ())],
+        6: [(6, 0, ())],
     })
-    forward_pass(3, 4, (0, 1), {5: [(5, 0, ())], 6: [(6, 0, ())]})
-    forward_pass(3, 4, (2, 3), {3: [(3, 1, (4,)), (4, 1, (5,))], 5: [(5, 1, ())], 6: [(6, 1, ())]})
+    forward_pass(2, 5, (2, 3), {3: [(3, 1, (4,)), (4, 1, (5,))], 5: [(5, 1, ())], 6: [(6, 1, ())]})
     forward_pass(7, 2, every, {7: [(7, 0, ()), (7, 1, ())], 8: [(8, 0, ()), (8, 1, ())]})
 
     for c in range(SPAN):
@@ -297,7 +310,6 @@
     relay((), (0, 1, 2))
 
     piece = D // GROUP
-    core = a % 2
     chips = GROUP // 2
     chip = (a // 2) * NH + b
 
@@ -323,12 +335,12 @@
         for j in range(1, chips):
             part_copy(j).start()
 
-    def backward_unit(slot):
+    def backward_unit(slot, tiles):
         factors = {
             (part, c): jnp.exp2((mb_s[slot, part, c] - m_s[c]) * EXPO) * rl_s[c]
-            for part in range(2) for c in near_queries((2 * part, 2 * part + 1))
+            for part in sorted({t // 2 for t in tiles}) for c in near_queries((2 * part, 2 * part + 1))
         }
-        for t in every:
+        for t in tiles:
             vals = jnp.concatenate([tile_of(kv_s, slot, 1, t), ones_cols], axis=1)
             for c in range(*queries_of(t)):
                 n = PAIR_AT[t, c]
@@ -336,7 +348,7 @@
                 probs = p_s[slot, n].astype(F32) * factors[t // 2, c]
                 ps_s[n] = probs.astype(BF16)
                 ds_s[n] = (probs * grad).astype(BF16)
-        for t in every:
+        for t in tiles:
             rows = slice((t % 2) * TILE, (t % 2 + 1) * TILE)
             lo, hi = queries_of(t)
             near = slice(lo * TILE, hi * TILE)
@@ -344,8 +356,8 @@
             many_ps = jnp.concatenate([ps_s[PAIR_AT[t, c]] for c in range(lo, hi)], axis=1)
             send_s[slot, t // 2, 0, rows] = (dot(many_ds, q_s[near]) * SCALE).astype(BF16)
             send_s[slot, t // 2, 1, rows] = dot(many_ps, do_s[near]).astype(BF16)
-        for c in range(SPAN):
-            lo, hi = keys_of(c, every)
+        for c in near_queries(tiles):
+            lo, hi = keys_of(c, tiles)
             many = jnp.concatenate([ds_s[PAIR_AT[t, c]] for t in range(lo, hi)], axis=0)
             dqt_s[c] += dot(kt_s[slot, :, lo * TILE:hi * TILE], many)
 
@@ -354,7 +366,11 @@
         (8, 0): (rd_s.at[1], 1, dev_cross, both(inner, has_hi), both(inner, has_hi)),
         (7, 1): (rx_s.at[0], 2, dev_lo, both(inner, has_lo), both(inner, has_hi)),
         (8, 1): (rx_s.at[1], 3, dev_hi, both(inner, has_hi), both(inner, has_lo)),
+        (7, 2): (rw_s.at[0], 16, dev_lo, both(inner, has_lo), both(inner, has_hi)),
+        (8, 2): (rw_s.at[1], 17, dev_hi, both(inner, has_hi), both(inner, has_lo)),
     }
+    inside = {0: (0, 0), 2: (0, 1)}
+
     for part in range(2):
         at = 4 + 6 * part
         back[5, part] = (rp_s.at[1, part], at, dev_partner, has_lo, has_lo)
@@ -366,77 +382,124 @@
     needs = {key: () for key in back}
     needs[3, 0], needs[4, 0] = ((5, 0), (7, 0)), ((6, 0), (8, 0))
     needs[3, 1], needs[4, 1] = ((5, 1),), ((6, 1),)
+    needs[2, 0] = ((7, 2), (8, 2))
     needs[2, 1] = ((7, 1), (8, 1))
 
     def back_copy(key):
         slot, part = key
         target, index, device, _, _ = back[key]
-        return remote(send_s.at[slot, part], target, b_send.at[index], b_recv.at[index], device)
+        source = send_s.at[(slot,) + inside[part]] if slot > 6 and part in inside else send_s.at[slot, part]
+        return remote(source, target, b_send.at[index], b_recv.at[index], device)
 
     def merge(key, source):
         @pl.when(back[source][4])
         def _():
             back_copy(source).wait_recv()
-            slot, part = key
+            at = (key[0],) + inside[source[1]] if source[0] > 6 and source[1] in inside else key
             arrived = back[source][0][...].astype(F32)
-            send_s[slot, part] = (send_s[slot, part].astype(F32) + arrived).astype(BF16)
-
-    def backward_step(i, carry):
-        slot = chosen(i, BACK_ORDER)
+            send_s[at] = (send_s[at].astype(F32) + arrived).astype(BF16)
+
+    def give_back(key, who):
+        @pl.when(both(who, back[key][3]))
+        def _():
+            for source in needs[key]:
+                merge(key, source)
+            back_copy(key).start()
+
+    outer = jnp.logical_not(inner)
+
+    def first_step(i, carry):
+        slot = jnp.where(inner, 7 + i, 3 + i)
+
+        @pl.when(exists(slot))
+        def _():
+            backward_unit(slot, every)
+
+        for n in (7, 8):
+            @pl.when(i == n - 7)
+            def _():
+                for part in range(3):
+                    give_back((n, part), inner)
+
+        return carry
+
+    lax.fori_loop(0, 2, first_step, 0)
+
+    for part in range(2):
+        def partner_step(i, carry):
+            if part == 1:
+                @pl.when(i == 1)
+                def _():
+                    relay((0,), (3, 4))
+
+            @pl.when(exists(i + 5))
+            def _():
+                backward_unit(i + 5, (2 * part, 2 * part + 1))
+
+            for n in (5, 6):
+                @pl.when(i == n - 5)
+                def _():
+                    give_back((n, part), yes)
+
+            return carry
+
+        lax.fori_loop(0, 2, partner_step, 0)
+        for n in (3, 4):
+            give_back((n, part), outer)
+
+    def last_step(i, carry):
+        slot = chosen(i, LAST_ORDER)
+        own_side = both(slot >= 3, outer)
+
+        @pl.when(i == 0)
+        def _():
+            relay((1, 2), (5, 6))
+
+        @pl.when(i == 3)
+        def _():
+            weight_product()
+            wgat_s[core, h] = w_s[weight_rows(h)]
+            for j in range(1, HEADS):
+                weight_copy(j).wait_recv()
+            weight_exchange().start()
 
         @pl.when(i == 4)
         def _():
-            relay((0,), (3, 4))
-            relay((1, 2), (5, 6))
-            weight_product()
-
-        @pl.when(i == 6)
-        def _():
             weight_parts()
-
-        @pl.when(i == 7)
-        def _():
             relay((3, 4), (7, 8))
 
-        @pl.when(exists(slot))
-        def _():
-            backward_unit(slot)
-
-        for n in range(1, SLOTS):
+        @pl.when(both(exists(slot), jnp.logical_not(own_side)))
+        def _():
+            backward_unit(slot, every)
+
+        for n in range(1, 5):
             @pl.when(slot == n)
             def _():
                 for part in range(2):
-                    @pl.when(back[n, part][3])
-                    def _():
-                        for source in needs[n, part]:
-                            merge((n, part), source)
-                        back_copy((n, part)).start()
+                    give_back((n, part), inner if n in (3, 4) else yes)
 
         return carry
 
-    lax.fori_loop(0, SLOTS, backward_step, 0)
+    lax.fori_loop(0, len(LAST_ORDER), last_step, 0)
 
     for c in range(SPAN):
         rows = slice(c * TILE, (c + 1) * TILE)
-        dq_ref[rows] = (dqt_s[c] * SCALE).T.astype(BF16)
-
-    loads_w = w_s[pl.ds(pl.multiple_of(h * share, share), share)]
-    wgat_s[h] = loads_w
-    for j in range(1, HEADS):
-        weight_copy(j).wait_recv()
-    relay((5, 6, 7, 8), ())
-    weights = jnp.concatenate([wgat_s[n] for n in range(HEADS)], axis=1)
-    everyone = jnp.concatenate([ag_s[n] for n in range(HEADS)], axis=0)
-    mixed_ref[...] = dot(weights, everyone).astype(BF16).reshape(share, SPAN, TILE)
-
-    red_s[chip] = sum_s[chip]
-    for j in range(1, chips):
-        part_copy(j).wait_recv()
-    total = red_s[0].astype(F32)
-    for n in range(1, chips):
-        total = total + red_s[n].astype(F32)
-    wg_ref[...] = total
-
+        dq_s[rows] = (dqt_s[c] * SCALE).T.astype(BF16)
+
+    stores = [
+        pltpu.make_async_copy(src, dst, out_sem.at[i])
+        for i, (src, dst) in enumerate(
+            [(mixed_s, mixed_ref), (dq_s, dq_ref), (dk_s, dk_ref), (dv_s, dv_ref), (wg_s, wg_ref)]
+        )
+    ]
+    stores[1].start()
+
+    def projected(heads):
+        rows = [jnp.concatenate([wgat_s[i, n] for n in heads], axis=1) for i in range(2)]
+        return dot(jnp.concatenate(rows, axis=0), jnp.concatenate([ag_s[n] for n in heads], axis=0))
+
+    weight_exchange().wait_recv()
+    most_s[...] = projected((h, side, up, down, side_up, side_down))
     for part in range(2):
         back_copy((1, part)).wait_recv()
         acc_s[part] = send_s[0, part].astype(F32) + rp_s[0, part].astype(F32)
@@ -447,8 +510,26 @@
                 back_copy((source, part)).wait_recv()
                 acc_s[part] += back[source, part][0][...].astype(F32)
         rows = slice(part * HALF, (part + 1) * HALF)
-        dk_ref[rows] = acc_s[part, 0].astype(BF16)
-        dv_ref[rows] = acc_s[part, 1].astype(BF16)
+        dk_s[rows] = acc_s[part, 0].astype(BF16)
+        dv_s[rows] = acc_s[part, 1].astype(BF16)
+
+    stores[2].start()
+    stores[3].start()
+
+    relay((5, 6, 7, 8), ())
+    far = (h + HEADS // 2) % HEADS
+    mixed = most_s[...] + projected((far, (side + HEADS // 2) % HEADS))
+    mixed_s[...] = mixed.astype(BF16).reshape(share, SPAN, TILE)
+    stores[0].start()
+
+    red_s[chip] = sum_s[chip]
+    for j in range(1, chips):
+        part_copy(j).wait_recv()
+    total = red_s[0].astype(F32)
+    for n in range(1, chips):
+        total = total + red_s[n].astype(F32)
+    wg_s[...] = total
+    stores[4].start()
 
     for n in range(len(hops)):
         @pl.when(hops[n][3])
@@ -459,6 +540,7 @@
         @pl.when(sends)
         def _():
             back_copy(key).wait_send()
+    weight_exchange().wait_send()
     for j in range(1, HEADS):
         weight_copy(j).wait_send()
     for n in range(len(gathers)):
@@ -466,6 +548,8 @@
     pair_copy().wait_send()
     for j in range(1, chips):
         part_copy(j).wait_send()
+    for store in stores:
+        store.wait()
 
 
 def hand_over(*refs):
@@ -483,7 +567,6 @@
 
 def per_device(queries, key_tiles, values, token_valid, out_weight, out_grad):
     any_spec = pl.BlockSpec(memory_space=pl.ANY)
-    vmem_spec = pl.BlockSpec(memory_space=pltpu.VMEM)
     vmem = pltpu.VMEM
     dma = pltpu.SemaphoreType.DMA
     token = jax.ShapeDtypeStruct((TOKENS, HD), BF16)
@@ -496,9 +579,16 @@
             token, token, token,
             jax.ShapeDtypeStruct((D // GROUP, HD), F32),
         ),
-        in_specs=[any_spec, any_spec, any_spec, vmem_spec, any_spec, any_spec],
-        out_specs=(vmem_spec,) * 5,
+        in_specs=[any_spec] * 6,
+        out_specs=(any_spec,) * 5,
         scratch_shapes=[
+            vmem((D // HEADS, SPAN, TILE), BF16),
+            vmem((D // HEADS, TOKENS), F32),
+            vmem((TOKENS, HD), BF16),
+            vmem((TOKENS, HD), BF16),
+            vmem((TOKENS, HD), BF16),
+            vmem((D // GROUP, HD), F32),
+            vmem((NT, NH, SPAN, TILE), jnp.int32),
             vmem((TOKENS, HD), BF16),
             vmem((SLOTS, 2) + unit, BF16),
             vmem((SLOTS, HD, TOKENS), BF16),
@@ -523,15 +613,16 @@
             vmem((3, 2) + unit, BF16),
             vmem((2, 2) + unit, BF16),
             vmem((2,) + unit, BF16),
-            vmem((2,) + unit, BF16),
+            vmem((2, HALF, HD), BF16),
+            vmem((2, HALF, HD), BF16),
             vmem((2,) + unit, BF16),
             vmem((HEADS, HD, TOKENS), BF16),
-            vmem((HEADS, D // HEADS, HD), BF16),
+            vmem((2, HEADS, D // HEADS // 2, HD), BF16),
             vmem((2,) + pieces, BF16),
             vmem(pieces, BF16),
             vmem(pieces, BF16),
             vmem(pieces, BF16),
-            dma((7,)), dma((10, 2)), dma((SLOTS, 2)), dma((16,)), dma((16,)),
+            dma((8,)), dma((5,)), dma((10, 2)), dma((SLOTS, 2)), dma((18,)), dma((18,)),
             dma((9,)), dma((9,)), dma((HEADS,)), dma((HEADS,)), dma((GROUP // 2,)), dma((GROUP // 2,)),
         ],
         compiler_params=pltpu.CompilerParams(

time: 59.2 us -> 56 us (0.946); the launches traced: 58.4 us -> 55.9 us
  Pallas kernels: 57.8 us -> 55.1 us
    pallas_call x1, Pallas kernels: 55.7 us -> 53 us  [per_device(): pl.pallas_call(kernel, out_shape=(jax.ShapeDtypeStruct((D // HEADS, SPAN,...]
where the time goes in v4:
time: 56 us; the launch traced here: 55.9 us
  Pallas kernels  55.1 us (98%)
  between operations  0.8 us (1%)
    pallas_call x1, Pallas kernels, per_device(): pl.pallas_call(kernel, out_shape=(jax.ShapeDtypeStruct((D // HEADS, SPAN,...  53 us
    pallas_call x1, Pallas kernels, per_device(): pl.pallas_call(hand_over, out_shape=[jax.ShapeDtypeStruct(r.shape, r.dtyp...  2.09 us

profile of v4, /device:TPU:1, one launch (start us, length us, event | category | flops | bytes accessed | tf_op | source)
XLA Modules:
  0.0 55.9 jit_solution(14655623532028854486)
XLA Ops:
  0.6 53.0 %shard_map.101 = (bf16[192,4,256]{2,1,0:T(4,128)(2,1)}, bf16[1024,128]{1,0:T(8,128)(2,1)}, bf16[1024,128]{1,0:T(8,128)(2,1)}, bf16[1024,128]{1,0:T(8,128)(2,1)}, f32[96,128]{1,0:T(8,128)}) custom-call(bf16[1024,128]{1,0:T(8,128)(2,1)} %bitcast.11, bf16[1024,128]{1,0:T(8,128)(2,1)} %bitcast.12, bf16[1024,128]{1,0:T(8,128)(2,1)} %bitcast.13, ...), custom_call_target="tpu_custom_call" | custom-call | tf_op jit(solution)/shard_map/pallas_call | solution.py:575
  53.6 2.1 %shard_map.102 = (bf16[192,4,256]{2,1,0:T(4,128)(2,1)}, bf16[1024,128]{1,0:T(8,128)(2,1)}, bf16[1024,128]{1,0:T(8,128)(2,1)}, bf16[1024,128]{1,0:T(8,128)(2,1)}, f32[96,128]{1,0:T(8,128)}) custom-call(bf16[192,4,256]{2,1,0:T(4,128)(2,1)} %get-tuple-element.15.refs_0_, bf16[1024,128]{1,0:T(8,128)(2,1)} %get-tuple-element.16.refs_1_, ...), custom_call_target="tpu_custom_call" | custom-call | tf_op jit(solution)/shard_map/pallas_call | solution.py:639

commit v5 on v4

--- a/solution.py
+++ b/solution.py
@@ -51,7 +51,7 @@
     q_s, kv_s, kt_s, vt_s, mask_s, w_s, raw_s, og_s,
     qt_s, do_s, dot_s, p_s, ps_s, ds_s, att_s, m_s, mb_s, rl_s, dqt_s,
     acc_s, send_s, rp_s, rz_s, rx_s, rd_s, rw_s, ry_s, ag_s, wgat_s, prod_s, pair_s, sum_s, red_s,
-    loc_sem, out_sem, f_send, f_recv, b_send, b_recv, ag_send, ag_recv, wt_send, wt_recv, pr_send, pr_recv,
+    loc_sem, f_send, f_recv, b_recv, ag_send, ag_recv, wt_send, wt_recv, pr_send, pr_recv,
 ):
     a = lax.axis_index("tm")
     b = lax.axis_index("height")
@@ -70,17 +70,15 @@
 
     loads = [
         pltpu.make_async_copy(src, dst, loc_sem.at[i])
-        for i, (src, dst) in enumerate(
-            [(q_ref, q_s), (w_ref, w_s), (og_ref, raw_s)]
-            + [
-                (ref.at[pl.ds(part * HALF, HALF)], kv_s.at[0, part, kind])
-                for part in range(2) for kind, ref in enumerate((k_ref, v_ref))
-            ]
-            + [(tv_ref, tv_s)]
-        )
+        for i, (src, dst) in enumerate([(q_ref, q_s), (tv_ref, tv_s), (w_ref, w_s), (og_ref, raw_s)])
     ]
-    for n in (3, 4, 5, 6, 0, 7, 1, 2):
-        loads[n].start()
+    for part in range(2):
+        for kind, ref in enumerate((k_ref, v_ref)):
+            pltpu.make_async_copy(
+                ref.at[pl.ds(part * HALF, HALF)], kv_s.at[0, part, kind], loc_sem.at[4]
+            ).start()
+    for load in loads:
+        load.start()
 
     barrier = pltpu.get_barrier_semaphore()
     for j in range(1, GROUP):
@@ -128,8 +126,7 @@
                 kv_s.at[slot, part], kv_s.at[slot, part], f_send.at[0, 0], f_recv.at[slot, part], dev_partner
             ).wait_recv()
 
-    for n in range(3, 7):
-        loads[n].wait()
+    pltpu.make_async_copy(kv_s.at[0], kv_s.at[0], loc_sem.at[4]).wait()
     for part in range(2):
         for n in range(4):
             start_hop(n, part)
@@ -145,17 +142,21 @@
     def weight_copy(j):
         peer = (h + j) % HEADS
         return remote(
-            w_ref.at[weight_rows(peer)], wgat_s.at[core, h], wt_send.at[j], wt_recv.at[j], (a, b, peer)
+            w_ref.at[weight_rows(peer)], wgat_s.at[core, h], wt_send.at[0], wt_recv.at[0], (a, b, peer)
         )
 
     def weight_exchange():
-        return remote(wgat_s.at[core], wgat_s.at[core], wt_send.at[0], wt_recv.at[0], dev_partner)
+        return remote(wgat_s.at[core], wgat_s.at[core], wt_send.at[1], wt_recv.at[1], dev_partner)
+
+    def weight_copies():
+        others = wgat_s.at[core, pl.ds(0, HEADS - 1)]
+        return remote(others, others, wt_send.at[0], wt_recv.at[0], dev_partner)
 
     for j in range(1, HEADS):
         weight_copy(j).start()
 
     loads[0].wait()
-    loads[7].wait()
+    loads[1].wait()
     first_row = (lax.broadcasted_iota(jnp.int32, (HD, TILE), 0) == 0).astype(BF16)
     for c in range(SPAN):
         rows = slice(c * TILE, (c + 1) * TILE)
@@ -223,7 +224,7 @@
             att_s[c] = att_s[c] * shrink[c] + dot(vals, weights)
 
     def grad_attended():
-        for load in loads[1:3]:
+        for load in loads[2:]:
             load.wait()
         for n in range(0, D, HD):
             og_s[n:n + HD] = raw_s[n:n + HD].reshape(HD, TOKENS)
@@ -319,14 +320,19 @@
     def part_copy(j):
         peer = (chip + j) % chips
         return remote(
-            sum_s.at[peer], red_s.at[chip], pr_send.at[j], pr_recv.at[j], ((peer // NH) * 2 + core, peer % NH, h)
+            sum_s.at[peer], red_s.at[chip], pr_send.at[1], pr_recv.at[1], ((peer // NH) * 2 + core, peer % NH, h)
         )
 
+    def part_copies():
+        others = red_s.at[pl.ds(0, chips - 1)]
+        return remote(others, others, pr_send.at[1], pr_recv.at[1], dev_partner)
+
     def weight_product():
-        for n in range(GROUP):
-            frame, row = n // NH, n % NH
-            value = dot(og_s[n * piece:(n + 1) * piece], ag_s[h], ((1,), (1,)))
-            prod_s[frame % 2, (frame // 2) * NH + row] = value.astype(BF16)
+        for frame in range(NT):
+            first = frame * NH * piece
+            value = dot(og_s[first:first + NH * piece], ag_s[h], ((1,), (1,))).astype(BF16)
+            for row in range(NH):
+                prod_s[frame % 2, (frame // 2) * NH + row] = value[row * piece:(row + 1) * piece]
         pair_copy().start()
 
     def weight_parts():
@@ -334,6 +340,14 @@
         sum_s[...] = (prod_s[core].astype(F32) + pair_s[...].astype(F32)).astype(BF16)
         for j in range(1, chips):
             part_copy(j).start()
+
+    for n in range(len(hops)):
+        @pl.when(hops[n][3])
+        def _():
+            for part in hops[n][4]:
+                hop_copy(n, part).wait_send()
+
+    weight_product()
 
     def backward_unit(slot, tiles):
         factors = {
@@ -389,7 +403,7 @@
         slot, part = key
         target, index, device, _, _ = back[key]
         source = send_s.at[(slot,) + inside[part]] if slot > 6 and part in inside else send_s.at[slot, part]
-        return remote(source, target, b_send.at[index], b_recv.at[index], device)
+        return remote(source, target, f_send.at[index // 2, index % 2], b_recv.at[index], device)
 
     def merge(key, source):
         @pl.when(back[source][4])
@@ -410,6 +424,10 @@
 
     def first_step(i, carry):
         slot = jnp.where(inner, 7 + i, 3 + i)
+
+        @pl.when(i == 1)
+        def _():
+            weight_parts()
 
         @pl.when(exists(slot))
         def _():
@@ -457,16 +475,19 @@
 
         @pl.when(i == 3)
         def _():
-            weight_product()
             wgat_s[core, h] = w_s[weight_rows(h)]
-            for j in range(1, HEADS):
-                weight_copy(j).wait_recv()
+            weight_copies().wait_recv()
             weight_exchange().start()
 
+            @pl.when(inner)
+            def _():
+                relay((3, 4), (7, 8))
+
         @pl.when(i == 4)
         def _():
-            weight_parts()
-            relay((3, 4), (7, 8))
+            @pl.when(outer)
+            def _():
+                relay((3, 4), (7, 8))
 
         @pl.when(both(exists(slot), jnp.logical_not(own_side)))
         def _():
@@ -487,7 +508,7 @@
         dq_s[rows] = (dqt_s[c] * SCALE).T.astype(BF16)
 
     stores = [
-        pltpu.make_async_copy(src, dst, out_sem.at[i])
+        pltpu.make_async_copy(src, dst, loc_sem.at[i])
         for i, (src, dst) in enumerate(
             [(mixed_s, mixed_ref), (dq_s, dq_ref), (dk_s, dk_ref), (dv_s, dv_ref), (wg_s, wg_ref)]
         )
@@ -523,31 +544,23 @@
     stores[0].start()
 
     red_s[chip] = sum_s[chip]
-    for j in range(1, chips):
-        part_copy(j).wait_recv()
+    part_copies().wait_recv()
     total = red_s[0].astype(F32)
     for n in range(1, chips):
         total = total + red_s[n].astype(F32)
     wg_s[...] = total
     stores[4].start()
 
-    for n in range(len(hops)):
-        @pl.when(hops[n][3])
-        def _():
-            for part in hops[n][4]:
-                hop_copy(n, part).wait_send()
     for key, (_, _, _, sends, _) in back.items():
         @pl.when(sends)
         def _():
             back_copy(key).wait_send()
     weight_exchange().wait_send()
-    for j in range(1, HEADS):
-        weight_copy(j).wait_send()
+    weight_copies().wait_send()
     for n in range(len(gathers)):
         gather_copy(n).wait_send()
     pair_copy().wait_send()
-    for j in range(1, chips):
-        part_copy(j).wait_send()
+    part_copies().wait_send()
     for store in stores:
         store.wait()
 
@@ -555,7 +568,7 @@
 def hand_over(*refs):
     sources, targets, staged, sem = refs[:5], refs[5:10], refs[10:15], refs[15]
     reads = [pltpu.make_async_copy(sources[i], staged[i], sem.at[i]) for i in range(5)]
-    writes = [pltpu.make_async_copy(staged[i], targets[i], sem.at[i + 5]) for i in range(5)]
+    writes = [pltpu.make_async_copy(staged[i], targets[i], sem.at[i]) for i in range(5)]
     for read in reads:
         read.start()
     for read, write in zip(reads, writes):
@@ -622,8 +635,8 @@
             vmem(pieces, BF16),
             vmem(pieces, BF16),
             vmem(pieces, BF16),
-            dma((8,)), dma((5,)), dma((10, 2)), dma((SLOTS, 2)), dma((18,)), dma((18,)),
-            dma((9,)), dma((9,)), dma((HEADS,)), dma((HEADS,)), dma((GROUP // 2,)), dma((GROUP // 2,)),
+            dma((5,)), dma((10, 2)), dma((SLOTS, 2)), dma((18,)),
+            dma((9,)), dma((9,)), dma((2,)), dma((2,)), dma((2,)), dma((2,)),
         ],
         compiler_params=pltpu.CompilerParams(
             collective_id=0, has_side_effects=True, vmem_limit_bytes=60 * 1024 * 1024
@@ -641,7 +654,7 @@
         out_shape=[jax.ShapeDtypeStruct(r.shape, r.dtype) for r in results],
         in_specs=[any_spec] * 5,
         out_specs=[any_spec] * 5,
-        scratch_shapes=[vmem(r.shape, r.dtype) for r in results] + [dma((10,))],
+        scratch_shapes=[vmem(r.shape, r.dtype) for r in results] + [dma((5,))],
     )(*results)
     tile_shape = (1, 1, 1, SPAN, TILE, HD)
     return (

time: 56 us -> 54 us (0.964)
  Pallas kernels: 55.1 us -> 53.1 us
    pallas_call x1, Pallas kernels: 53 us -> 51.1 us  [per_device(): pl.pallas_call(kernel, out_shape=(jax.ShapeDtypeStruct((D // HEADS, SPAN,...]
where the time goes in v5:
time: 54 us; the launch traced here: 53.9 us
  Pallas kernels  53.1 us (98%)
  between operations  0.8 us (1%)
    pallas_call x1, Pallas kernels, per_device(): pl.pallas_call(kernel, out_shape=(jax.ShapeDtypeStruct((D // HEADS, SPAN,...  51.1 us
    pallas_call x1, Pallas kernels, per_device(): pl.pallas_call(hand_over, out_shape=[jax.ShapeDtypeStruct(r.shape, r.dtyp...  2.05 us

profile of v5, /device:TPU:1, one launch (start us, length us, event | category | flops | bytes accessed | tf_op | source)
XLA Modules:
  0.0 53.9 jit_solution(1824790878670374886)
XLA Ops:
  0.6 51.1 %shard_map.101 = (bf16[192,4,256]{2,1,0:T(4,128)(2,1)}, bf16[1024,128]{1,0:T(8,128)(2,1)}, bf16[1024,128]{1,0:T(8,128)(2,1)}, bf16[1024,128]{1,0:T(8,128)(2,1)}, f32[96,128]{1,0:T(8,128)}) custom-call(bf16[1024,128]{1,0:T(8,128)(2,1)} %bitcast.11, bf16[1024,128]{1,0:T(8,128)(2,1)} %bitcast.12, bf16[1024,128]{1,0:T(8,128)(2,1)} %bitcast.13, ...), custom_call_target="tpu_custom_call" | custom-call | tf_op jit(solution)/shard_map/pallas_call | solution.py:588
  51.7 2.0 %shard_map.102 = (bf16[192,4,256]{2,1,0:T(4,128)(2,1)}, bf16[1024,128]{1,0:T(8,128)(2,1)}, bf16[1024,128]{1,0:T(8,128)(2,1)}, bf16[1024,128]{1,0:T(8,128)(2,1)}, f32[96,128]{1,0:T(8,128)}) custom-call(bf16[192,4,256]{2,1,0:T(4,128)(2,1)} %get-tuple-element.15.refs_0_, bf16[1024,128]{1,0:T(8,128)(2,1)} %get-tuple-element.16.refs_1_, ...), custom_call_target="tpu_custom_call" | custom-call | tf_op jit(solution)/shard_map/pallas_call | solution.py:652

commit v6 on v5

--- a/solution.py
+++ b/solution.py
@@ -27,7 +27,7 @@
 
 SLOTS = 9
 HALF = TOKENS // 2
-LAST_ORDER = (2, 3, 4, 1, 0)
+LAST_ORDER = (3, 2, 4, 1, 0)
 
 PAIRS = [(k, q) for k in range(SPAN) for q in range(SPAN) if abs(k - q) <= 1]
 PAIR_AT = {pair: i for i, pair in enumerate(PAIRS)}
@@ -57,6 +57,7 @@
     b = lax.axis_index("height")
     h = lax.axis_index("head")
     inner = jnp.logical_or(a == 1, a == 2)
+    outer = jnp.logical_not(inner)
     has_lo = b > 0
     has_hi = b < NH - 1
     partner = a + 1 - 2 * (a % 2)
@@ -328,12 +329,14 @@
         return remote(others, others, pr_send.at[1], pr_recv.at[1], dev_partner)
 
     def weight_product():
-        for frame in range(NT):
-            first = frame * NH * piece
-            value = dot(og_s[first:first + NH * piece], ag_s[h], ((1,), (1,))).astype(BF16)
-            for row in range(NH):
-                prod_s[frame % 2, (frame // 2) * NH + row] = value[row * piece:(row + 1) * piece]
-        pair_copy().start()
+        for of in (1 - core, core):
+            for pair in range(NT // 2):
+                first = pl.multiple_of((2 * pair + of) * NH * piece, NH * piece)
+                value = dot(og_s[pl.ds(first, NH * piece)], ag_s[h], ((1,), (1,))).astype(BF16)
+                for row in range(NH):
+                    prod_s[of, pair * NH + row] = value[row * piece:(row + 1) * piece]
+            if of is not core:
+                pair_copy().start()
 
     def weight_parts():
         pair_copy().wait_recv()
@@ -348,6 +351,10 @@
                 hop_copy(n, part).wait_send()
 
     weight_product()
+
+    @pl.when(inner)
+    def _():
+        weight_parts()
 
     def backward_unit(slot, tiles):
         factors = {
@@ -420,12 +427,10 @@
                 merge(key, source)
             back_copy(key).start()
 
-    outer = jnp.logical_not(inner)
-
     def first_step(i, carry):
         slot = jnp.where(inner, 7 + i, 3 + i)
 
-        @pl.when(i == 1)
+        @pl.when(both(i == 1, outer))
         def _():
             weight_parts()
 
@@ -443,10 +448,14 @@
 
     lax.fori_loop(0, 2, first_step, 0)
 
+    @pl.when(outer)
+    def _():
+        relay((0,), (3, 4))
+
     for part in range(2):
         def partner_step(i, carry):
             if part == 1:
-                @pl.when(i == 1)
+                @pl.when(both(i == 1, inner))
                 def _():
                     relay((0,), (3, 4))
 
@@ -464,12 +473,16 @@
         lax.fori_loop(0, 2, partner_step, 0)
         for n in (3, 4):
             give_back((n, part), outer)
+        if part == 0:
+            @pl.when(outer)
+            def _():
+                relay((1, 2), (5, 6))
 
     def last_step(i, carry):
         slot = chosen(i, LAST_ORDER)
         own_side = both(slot >= 3, outer)
 
-        @pl.when(i == 0)
+        @pl.when(both(i == 0, inner))
         def _():
             relay((1, 2), (5, 6))
 
@@ -479,15 +492,9 @@
             weight_copies().wait_recv()
             weight_exchange().start()
 
-            @pl.when(inner)
-            def _():
-                relay((3, 4), (7, 8))
-
         @pl.when(i == 4)
         def _():
-            @pl.when(outer)
-            def _():
-                relay((3, 4), (7, 8))
+            relay((3, 4), (7, 8))
 
         @pl.when(both(exists(slot), jnp.logical_not(own_side)))
         def _():
@@ -524,6 +531,12 @@
     for part in range(2):
         back_copy((1, part)).wait_recv()
         acc_s[part] = send_s[0, part].astype(F32) + rp_s[0, part].astype(F32)
+    relay((5, 6, 7, 8), ())
+    far = (h + HEADS // 2) % HEADS
+    mixed = most_s[...] + projected((far, (side + HEADS // 2) % HEADS))
+    mixed_s[...] = mixed.astype(BF16).reshape(share, SPAN, TILE)
+    stores[0].start()
+
     for part in range(2):
         for source in (4, 3, 2):
             @pl.when(back[source, part][4])
@@ -536,12 +549,6 @@
 
     stores[2].start()
     stores[3].start()
-
-    relay((5, 6, 7, 8), ())
-    far = (h + HEADS // 2) % HEADS
-    mixed = most_s[...] + projected((far, (side + HEADS // 2) % HEADS))
-    mixed_s[...] = mixed.astype(BF16).reshape(share, SPAN, TILE)
-    stores[0].start()
 
     red_s[chip] = sum_s[chip]
     part_copies().wait_recv()

time: 54 us -> 53 us (0.981)
  Pallas kernels: 53.1 us -> 52.1 us
    pallas_call x1, Pallas kernels: 51.1 us -> 50.1 us  [per_device(): pl.pallas_call(kernel, out_shape=(jax.ShapeDtypeStruct((D // HEADS, SPAN,...]
where the time goes in v6:
time: 53 us; the launch traced here: 52.9 us
  Pallas kernels  52.1 us (98%)
  between operations  0.8 us (2%)
    pallas_call x1, Pallas kernels, per_device(): pl.pallas_call(kernel, out_shape=(jax.ShapeDtypeStruct((D // HEADS, SPAN,...  50.1 us
    pallas_call x1, Pallas kernels, per_device(): pl.pallas_call(hand_over, out_shape=[jax.ShapeDtypeStruct(r.shape, r.dtyp...  2.05 us

profile of v6, /device:TPU:1, one launch (start us, length us, event | category | flops | bytes accessed | tf_op | source)
XLA Modules:
  0.0 52.9 jit_solution(14310551181440973580)
XLA Ops:
  0.6 50.1 %shard_map.101 = (bf16[192,4,256]{2,1,0:T(4,128)(2,1)}, bf16[1024,128]{1,0:T(8,128)(2,1)}, bf16[1024,128]{1,0:T(8,128)(2,1)}, bf16[1024,128]{1,0:T(8,128)(2,1)}, f32[96,128]{1,0:T(8,128)}) custom-call(bf16[1024,128]{1,0:T(8,128)(2,1)} %bitcast.11, bf16[1024,128]{1,0:T(8,128)(2,1)} %bitcast.12, bf16[1024,128]{1,0:T(8,128)(2,1)} %bitcast.13, ...), custom_call_target="tpu_custom_call" | custom-call | tf_op jit(solution)/shard_map/pallas_call | solution.py:595
  50.7 2.0 %shard_map.102 = (bf16[192,4,256]{2,1,0:T(4,128)(2,1)}, bf16[1024,128]{1,0:T(8,128)(2,1)}, bf16[1024,128]{1,0:T(8,128)(2,1)}, bf16[1024,128]{1,0:T(8,128)(2,1)}, f32[96,128]{1,0:T(8,128)}) custom-call(bf16[192,4,256]{2,1,0:T(4,128)(2,1)} %get-tuple-element.15.refs_0_, bf16[1024,128]{1,0:T(8,128)(2,1)} %get-tuple-element.16.refs_1_, ...), custom_call_target="tpu_custom_call" | custom-call | tf_op jit(solution)/shard_map/pallas_call | solution.py:659

commit v7 on v6

--- a/solution.py
+++ b/solution.py
@@ -127,10 +127,16 @@
                 kv_s.at[slot, part], kv_s.at[slot, part], f_send.at[0, 0], f_recv.at[slot, part], dev_partner
             ).wait_recv()
 
-    pltpu.make_async_copy(kv_s.at[0], kv_s.at[0], loc_sem.at[4]).wait()
     for part in range(2):
         for n in range(4):
-            start_hop(n, part)
+            @pl.when(hops[n][3])
+            def _():
+                _, target, device, _, _ = hops[n]
+                for kind, ref in enumerate((k_ref, v_ref)):
+                    remote(
+                        ref.at[pl.ds(part * HALF, HALF)], kv_s.at[target, part, kind],
+                        f_send.at[n, part], f_recv.at[target, part], device,
+                    ).start()
 
     share = D // HEADS
 
@@ -158,6 +164,7 @@
 
     loads[0].wait()
     loads[1].wait()
+    pltpu.make_async_copy(kv_s.at[0], kv_s.at[0], loc_sem.at[4]).wait()
     first_row = (lax.broadcasted_iota(jnp.int32, (HD, TILE), 0) == 0).astype(BF16)
     for c in range(SPAN):
         rows = slice(c * TILE, (c + 1) * TILE)
@@ -546,9 +553,9 @@
         rows = slice(part * HALF, (part + 1) * HALF)
         dk_s[rows] = acc_s[part, 0].astype(BF16)
         dv_s[rows] = acc_s[part, 1].astype(BF16)
-
-    stores[2].start()
-    stores[3].start()
+        for kind, target in ((0, dk_ref), (1, dv_ref)):
+            pltpu.make_async_copy((dk_s, dv_s)[kind].at[rows], target.at[rows], loc_sem.at[2 + kind]).start()
+
 
     red_s[chip] = sum_s[chip]
     part_copies().wait_recv()

time: 53 us -> 53.2 us (level)
  no operation moved by 1% of the time
where the time goes in v7:
time: 53.2 us; the launch traced here: 53 us
  Pallas kernels  52.2 us (98%)
  between operations  0.8 us (2%)
    pallas_call x1, Pallas kernels, per_device(): pl.pallas_call(kernel, out_shape=(jax.ShapeDtypeStruct((D // HEADS, SPAN,...  50.2 us
    pallas_call x1, Pallas kernels, per_device(): pl.pallas_call(hand_over, out_shape=[jax.ShapeDtypeStruct(r.shape, r.dtyp...  2.05 us

profile of v7, /device:TPU:1, one launch (start us, length us, event | category | flops | bytes accessed | tf_op | source)
XLA Modules:
  0.0 53.0 jit_solution(12290799570477841213)
XLA Ops:
  0.6 50.2 %shard_map.101 = (bf16[192,4,256]{2,1,0:T(4,128)(2,1)}, bf16[1024,128]{1,0:T(8,128)(2,1)}, bf16[1024,128]{1,0:T(8,128)(2,1)}, bf16[1024,128]{1,0:T(8,128)(2,1)}, f32[96,128]{1,0:T(8,128)}) custom-call(bf16[1024,128]{1,0:T(8,128)(2,1)} %bitcast.11, bf16[1024,128]{1,0:T(8,128)(2,1)} %bitcast.12, bf16[1024,128]{1,0:T(8,128)(2,1)} %bitcast.13, ...), custom_call_target="tpu_custom_call" | custom-call | tf_op jit(solution)/shard_map/pallas_call | solution.py:602
  50.8 2.0 %shard_map.102 = (bf16[192,4,256]{2,1,0:T(4,128)(2,1)}, bf16[1024,128]{1,0:T(8,128)(2,1)}, bf16[1024,128]{1,0:T(8,128)(2,1)}, bf16[1024,128]{1,0:T(8,128)(2,1)}, f32[96,128]{1,0:T(8,128)}) custom-call(bf16[192,4,256]{2,1,0:T(4,128)(2,1)} %get-tuple-element.15.refs_0_, bf16[1024,128]{1,0:T(8,128)(2,1)} %get-tuple-element.16.refs_1_, ...), custom_call_target="tpu_custom_call" | custom-call | tf_op jit(solution)/shard_map/pallas_call | solution.py:666
